TPU v7x, 32 devices: a whole 2x2x4 slice. The times are simulated.
32 devices in a mesh: fsdp: 16 (over z, x, core), tensor: 2 (over y).
Axes of the slice: x: 2, y: 2, z: 4, core: 2. Of those that a mesh axis runs over, the one named last changes fastest.
Arguments:
- hidden_in: bfloat16 [8192, 5120], P('fsdp', 'tensor'), may hold values from -80 to 80
- norm_gain: bfloat16 [5120], replicated, may hold values from 0.099609375 to 1.8984375
- query_weight: bfloat16 [5120, 5120], P(('fsdp', 'tensor')), may hold values from -0.078125 to 0.078125
- key_weight: bfloat16 [5120, 1024], P(('fsdp', 'tensor')), may hold values from -0.078125 to 0.078125
- value_weight: bfloat16 [5120, 1024], P(('fsdp', 'tensor')), may hold values from -0.078125 to 0.078125
- out_weight: bfloat16 [5120, 5120], P(('fsdp', 'tensor')), may hold values from -0.078125 to 0.078125
- query_bias: bfloat16 [5120], P('tensor'), may hold values from -10.5 to 10.5
- key_bias: bfloat16 [1024], P('tensor'), may hold values from -5.5 to 5.5
- value_bias: bfloat16 [1024], P('tensor'), may hold values from -3 to 3
- span_start: int32 [32], P('fsdp'), may hold values from 0 to 3839
- span_length: int32 [32], P('fsdp'), may hold values from 64 to 256, as said below
Outputs:
- attention_out: bfloat16 [8192, 5120], P('fsdp', 'tensor')
- key_cache: bfloat16 [8192, 1024], P('fsdp', 'tensor')
- value_cache: bfloat16 [8192, 1024], P('fsdp', 'tensor')
Inputs may be any that keep to these rules, and one draw needn't show every extreme that they name: `span_length`: the spans of the first rollout group are all full.
All inputs are finite; a program needn't handle non-finite values.
Results may differ from a plain program's by a relative error of at most 0.0065.
The roundings to bfloat16 on the way count: a program that leaves them out, or rounds other values in their place, can miss the bound.
Values may be sent and summed in bfloat16 or wider, within the bound.
A program may use at most 192 MiB of HBM per device.

v0:
```python
import jax
import jax.numpy as jnp
from jax import lax
from jax.sharding import PartitionSpec as P

HEADS = 40
KV_HEADS = 8
HEAD = 128


rope_base = 1000000.0
epsilon = 1e-06


def rotate(entries, cosine, sine):
    half = entries.shape[-1] // 2
    first = entries[..., :half]
    second = entries[..., half:]
    return jnp.concatenate(
        [first * cosine - second * sine, second * cosine + first * sine], axis=-1
    )


def angles(span_start, span_size):
    positions = span_start[:, None] + jnp.arange(span_size, dtype=jnp.int32)[None, :]
    inverse = 1.0 / rope_base ** (jnp.arange(0, HEAD, 2, dtype=jnp.float32) / HEAD)
    phase = positions.reshape(-1).astype(jnp.float32)[:, None] * inverse[None, :]
    return (jnp.cos(phase)[:, None, :], jnp.sin(phase)[:, None, :])


def local(
    hidden_in,
    norm_gain,
    query_weight,
    key_weight,
    value_weight,
    out_weight,
    query_bias,
    key_bias,
    value_bias,
    span_start,
    span_length,
):
    slices = lax.axis_size("tensor")
    members = lax.axis_size("fsdp")
    token_rows = hidden_in.shape[0]
    local_spans = span_start.shape[0]
    span_size = token_rows // local_spans
    query_cols = query_weight.shape[1] // slices
    key_cols = key_weight.shape[1] // slices
    learner_rows = query_weight.shape[0]
    gathered = lax.all_gather(hidden_in, "tensor", axis=1, tiled=True)
    source = gathered.astype(jnp.float32)
    inverse_rms = lax.rsqrt(jnp.mean(source * source, axis=-1, keepdims=True) + epsilon)
    normed = (source * inverse_rms * norm_gain.astype(jnp.float32)).astype(jnp.bfloat16)
    joined = jnp.concatenate(
        [
            query_weight.reshape(learner_rows, slices, query_cols),
            key_weight.reshape(learner_rows, slices, key_cols),
            value_weight.reshape(learner_rows, slices, key_cols),
        ],
        axis=2,
    )
    joined_cols = joined.shape[2]
    tiled = jnp.broadcast_to(
        jnp.transpose(joined, (1, 0, 2))[None], (members, slices, learner_rows, joined_cols)
    )
    tiled = tiled.reshape(members * slices, learner_rows, joined_cols)
    arrived = lax.all_to_all(tiled, ("fsdp", "tensor"), split_axis=0, concat_axis=0, tiled=True)
    projected = jnp.dot(
        normed, arrived.reshape(-1, joined_cols), preferred_element_type=jnp.float32
    )
    query = projected[:, :query_cols] + query_bias.astype(jnp.float32)
    keys = projected[:, query_cols : query_cols + key_cols] + key_bias.astype(jnp.float32)
    values = projected[:, query_cols + key_cols :] + value_bias.astype(jnp.float32)
    local_heads = query_cols // HEAD
    local_kv = key_cols // HEAD
    groups = HEADS // KV_HEADS
    cosine, sine = angles(span_start, span_size)
    query = rotate(query.reshape(token_rows, local_heads, HEAD), cosine, sine).astype(jnp.bfloat16)
    keys = rotate(keys.reshape(token_rows, local_kv, HEAD), cosine, sine)
    live = (jnp.arange(span_size, dtype=jnp.int32)[None, :] < span_length[:, None]).reshape(
        token_rows, 1, 1
    )
    key_cache = jnp.where(live, keys, 0.0).astype(jnp.bfloat16)
    value_cache = jnp.where(live, values.reshape(token_rows, local_kv, HEAD), 0.0).astype(
        jnp.bfloat16
    )
    query_blocks = query.reshape(local_spans, span_size, local_kv, groups, HEAD)
    key_blocks = key_cache.reshape(local_spans, span_size, local_kv, HEAD)
    value_blocks = value_cache.reshape(local_spans, span_size, local_kv, HEAD)
    scores = jnp.einsum(
        "sqkgd,stkd->skgqt", query_blocks, key_blocks, preferred_element_type=jnp.float32
    ) * HEAD ** (-0.5)
    rows = jnp.arange(span_size, dtype=jnp.int32)[:, None]
    columns = jnp.arange(span_size, dtype=jnp.int32)[None, :]
    allowed = (columns <= rows)[None] & (columns[None] < span_length[:, None, None])
    scores = jnp.where(allowed[:, None, None], scores, -1e30)
    highest = jnp.max(scores, axis=-1, keepdims=True)
    raised = jnp.exp(scores - highest)
    probs = (raised / jnp.sum(raised, axis=-1, keepdims=True)).astype(jnp.bfloat16)
    mixed = jnp.einsum("skgqt,stkd->sqkgd", probs, value_blocks, preferred_element_type=jnp.float32)
    attended = mixed.reshape(token_rows, local_heads * HEAD).astype(jnp.bfloat16)
    all_heads = lax.all_gather(attended, "tensor", axis=1, tiled=True)
    out_rows_local = out_weight.shape[0]
    out_cols = out_weight.shape[1] // slices
    out_block = out_weight.reshape(out_rows_local, slices, out_cols)
    tiled_out = jnp.broadcast_to(
        jnp.transpose(out_block, (1, 0, 2))[None], (members, slices, out_rows_local, out_cols)
    )
    tiled_out = tiled_out.reshape(members * slices, out_rows_local, out_cols)
    arrived_out = lax.all_to_all(
        tiled_out, ("fsdp", "tensor"), split_axis=0, concat_axis=0, tiled=True
    )
    combined = jnp.dot(
        all_heads, arrived_out.reshape(-1, out_cols), preferred_element_type=jnp.float32
    )
    attention_out = combined.astype(jnp.bfloat16)
    return (
        attention_out,
        key_cache.reshape(token_rows, local_kv * HEAD),
        value_cache.reshape(token_rows, local_kv * HEAD),
    )


def solution(mesh):
    placed = (
        P("fsdp", "tensor"),
        P(),
        P(("fsdp", "tensor"), None),
        P(("fsdp", "tensor"), None),
        P(("fsdp", "tensor"), None),
        P(("fsdp", "tensor"), None),
        P("tensor"),
        P("tensor"),
        P("tensor"),
        P("fsdp"),
        P("fsdp"),
    )
    return jax.shard_map(
        local,
        mesh=mesh,
        in_specs=placed,
        out_specs=(P("fsdp", "tensor"), P("fsdp", "tensor"), P("fsdp", "tensor")),
        check_vma=False,
    )
```

profile of v0, /device:TPU:0, one launch (start us, length us, event | category | flops | bytes accessed | tf_op | source)
XLA Modules:
  0.0 1475.6 jit_solution(9228143562208170029)
XLA Ops:
  9.6 4.2 reshape.193
  16.2 12.0 broadcast_in_dim.33
  28.2 7.4 all-to-all-start
  37.0 803.4 %all-to-all-done = bf16[32,160,3584]{2,1,0:T(8,128)(2,1)} async-done(((bf16[32,160,3584]{2,1,0:T(8,128)(2,1)}), bf16[32,160,3584]{2,1,0:T(8,128)(2,1)}, u32[]{:S(2)}, u32[]{:S(2)}) %all-to-all-start) | async-done | bytes 36700192 | tf_op jit(solution)/shard_map/all_to_all | solution.py:69
  840.4 8.8 broadcast_in_dim.41
  849.2 22.8 %all-to-all-start.1 = ((bf16[32,160,2560]{2,1,0:T(8,128)(2,1)}), bf16[32,160,2560]{2,1,0:T(8,128)(2,1)}, u32[]{:S(2)}, u32[]{:S(2)}) async-start(bf16[32,160,2560]{2,1,0:T(8,128)(2,1)} %bitcast.47), calls=%async_computation.1 | async-start | bytes 52428800 | tf_op jit(solution)/shard_map/all_to_all | solution.py:112
  874.0 212.8 %all-gather.3.cloned.1.call-done = bf16[512,5120]{1,0:T(8,128)(2,1)} async-done(((bf16[512,2560]{1,0:T(8,128)(2,1)}), bf16[512,5120]{1,0:T(8,128)(2,1)}) %all-gather.3.cloned.1.call-update) | async-done | bytes 5242896 | tf_op jit(solution)/shard_map/all_gather | solution.py:52
  1086.8 3.7 fusion.1
  1090.8 23.4 %fusion.5 = f32[512,3584]{1,0:T(8,128)S(1)} fusion(bf16[5120,3584]{1,0:T(8,128)(2,1)} %bitcast.2, bf16[512,5120]{1,0:T(8,128)(2,1)S(1)} %copy-done.1, f32[5120]{0:T(1024)S(1)} %convert_element_type.60, f32[512]{0:T(512)S(1)} %add_rsqrt_fusion), kind=kOutput, calls=%fused_computation.10 | convolution fusion | flops 18800967680 | bytes 49305600 | tf_op jit(solution)/shard_map/dot_general | solution.py:70
  1114.2 2.9 copy-done
  1117.2 2.8 slice_add_fusion
  1120.0 5.9 copy.23
  1125.9 4.5 subtract_convert_fusion
  1131.7 3.8 copy.25
  1135.5 4.0 concatenate.28
  1139.5 4.7 copy.24
  1144.2 2.4 slice_add_fusion.1
  1146.6 2.6 copy.40
  1153.6 2.6 select_convert_fusion
  1160.7 7.8 fusion.13
  1168.4 11.1 fusion.25
  1180.6 2.7 copy.29
  1185.2 262.1 %all-to-all-done.1 = bf16[32,160,2560]{2,1,0:T(8,128)(2,1)} async-done(((bf16[32,160,2560]{2,1,0:T(8,128)(2,1)}), bf16[32,160,2560]{2,1,0:T(8,128)(2,1)}, u32[]{:S(2)}, u32[]{:S(2)}) %all-to-all-start.1) | async-done | bytes 26214432 | tf_op jit(solution)/shard_map/all_to_all | solution.py:112
  1447.4 21.4 %convolution_convert_fusion = bf16[512,2560]{1,0:T(8,128)(2,1)} fusion(bf16[512,5120]{0,1:T(8,128)(2,1)} %all-gather.5.cloned.1.call-done, bf16[5120,2560]{1,0:T(8,128)(2,1)} %bitcast.10), kind=kOutput, calls=%fused_computation.18 | convolution fusion | flops 13423083520 | bytes 34078720 | tf_op jit(solution)/shard_map/dot_general | solution.py:115
  (52 shorter events, 21.4 us)
Async XLA Ops:
  28.2 7.4 copy-start.2
  28.2 812.2 %all-to-all-start = ((bf16[32,160,3584]{2,1,0:T(8,128)(2,1)}), bf16[32,160,3584]{2,1,0:T(8,128)(2,1)}, u32[]{:S(2)}, u32[]{:S(2)}) async-start(bf16[32,160,3584]{2,1,0:T(8,128)(2,1)} %bitcast.46), calls=%async_computation | async-start | bytes 73400320 | tf_op jit(solution)/shard_map/all_to_all | solution.py:69
  849.2 23.8 %copy-start.3 = (bf16[5120]{0:T(1024)(128)(2,1)S(1)}, bf16[5120]{0:T(1024)(128)(2,1)}, u32[]{:S(2)}) copy-start(bf16[5120]{0:T(1024)(128)(2,1)} %param.12) | copy-start | bytes 30724
  849.2 23.8 %copy-start.4 = (bf16[2560]{0:T(1024)(128)(2,1)S(1)}, bf16[2560]{0:T(1024)(128)(2,1)}, u32[]{:S(2)}) copy-start(bf16[2560]{0:T(1024)(128)(2,1)} %param.17) | copy-start | bytes 15364
  849.2 23.8 %copy-start.7 = (s32[2]{0:T(128)S(1)}, s32[2]{0:T(128)}, u32[]{:S(2)}) copy-start(s32[2]{0:T(128)} %param.20) | copy-start | bytes 28
  849.2 23.9 %copy-start.8 = (s32[2]{0:T(128)S(1)}, s32[2]{0:T(128)}, u32[]{:S(2)}) copy-start(s32[2]{0:T(128)} %param.21) | copy-start | bytes 28
  849.2 24.0 %copy-start.5 = (bf16[512]{0:T(512)(128)(2,1)S(1)}, bf16[512]{0:T(512)(128)(2,1)}, u32[]{:S(2)}) copy-start(bf16[512]{0:T(512)(128)(2,1)} %param.19) | copy-start | bytes 3076
  849.2 24.0 %copy-start.6 = (bf16[512]{0:T(512)(128)(2,1)S(1)}, bf16[512]{0:T(512)(128)(2,1)}, u32[]{:S(2)}) copy-start(bf16[512]{0:T(512)(128)(2,1)} %param.18) | copy-start | bytes 3076
  849.2 598.1 %all-to-all-start.1 = ((bf16[32,160,2560]{2,1,0:T(8,128)(2,1)}), bf16[32,160,2560]{2,1,0:T(8,128)(2,1)}, u32[]{:S(2)}, u32[]{:S(2)}) async-start(bf16[32,160,2560]{2,1,0:T(8,128)(2,1)} %bitcast.47), calls=%async_computation.1 | async-start | bytes 52428800 | tf_op jit(solution)/shard_map/all_to_all | solution.py:112
  872.0 214.8 %all-gather.3.cloned.1.call-start = ((), (), s32[]{:S(2)}) async-start(), calls=%async_computation.2 | async-start | bytes 7864320 | tf_op jit(solution)/shard_map/all_gather | solution.py:52
  872.8 574.6 %all-gather.5.cloned.1.call-start = ((), (), s32[]{:S(2)}) async-start(), calls=%async_computation.3 | async-start | bytes 7864320 | tf_op jit(solution)/shard_map/all_gather | solution.py:104
  1086.8 4.0 copy-start.1
  1114.2 2.9 copy-start
Sparse Core Ops, SparseCore 0:
  874.4 212.3 all-gather.2
  1185.4 155.9 all-gather.4
where the time goes:
time: 1490 us; the launch traced here: 1480 us
  waiting for transfers between devices  1280 us (86%)
  local copies, waits for them, and re-layouts  63.8 us (4%)
  matrix products  53.5 us (4%)
  other arithmetic  34.5 us (2%)
  starting transfers between devices  30.4 us (2%)
    all_to_all x1, waiting for transfers between devices, local(): lax.all_to_all(tiled, ('fsdp', 'tensor'), split_axis=0, concat_axis=0, ti...  803 us
    all_to_all x1, waiting for transfers between devices, local(): lax.all_to_all(tiled_out, ('fsdp', 'tensor'), split_axis=0, concat_axis=0...  262 us
    all_gather x1, waiting for transfers between devices, local(): gathered = lax.all_gather(hidden_in, 'tensor', axis=1, tiled=True)  213 us
  transfers between devices with their start and end apart: 4, of which 3 were waited for; matrix products, arithmetic and copies ran while one was open for 7% of the time, Pallas kernels for 0%

commit v1 on v0

v1 whole, which is shorter than its diff:
```python
import jax
import jax.numpy as jnp
from jax import lax
from jax.sharding import PartitionSpec as P

HEADS = 40
KV_HEADS = 8
HEAD = 128
GROUPS = HEADS // KV_HEADS
AXES = ("fsdp", "tensor")

rope_base = 1000000.0
epsilon = 1e-06


def rotate(entries, cosine, sine):
    half = entries.shape[-1] // 2
    first = entries[..., :half]
    second = entries[..., half:]
    return jnp.concatenate(
        [first * cosine - second * sine, second * cosine + first * sine], axis=-1
    )


def angles(span_start, span_size):
    positions = span_start[:, None] + jnp.arange(span_size, dtype=jnp.int32)[None, :]
    inverse = 1.0 / rope_base ** (jnp.arange(0, HEAD, 2, dtype=jnp.float32) / HEAD)
    phase = positions.reshape(-1).astype(jnp.float32)[:, None] * inverse[None, :]
    return (jnp.cos(phase)[:, None, :], jnp.sin(phase)[:, None, :])


def local(
    hidden_in,
    norm_gain,
    query_weight,
    key_weight,
    value_weight,
    out_weight,
    query_bias,
    key_bias,
    value_bias,
    span_start,
    span_length,
):
    slices = lax.axis_size("tensor")
    members = lax.axis_size("fsdp")
    devices = slices * members
    inner = KV_HEADS // slices
    outer = devices // KV_HEADS
    line = lax.axis_index("fsdp") // inner
    i = lax.axis_index("fsdp") % inner
    t = lax.axis_index("tensor")
    token_rows, features = hidden_in.shape
    local_spans = span_start.shape[0]
    span_size = token_rows // local_spans
    learner_rows = query_weight.shape[0]
    qc = GROUPS * HEAD
    oc = out_weight.shape[1] // KV_HEADS

    def xor(x, k):
        return lax.ppermute(x, AXES, [(d, d ^ k) for d in range(devices)])

    def shift(x, step):
        pairs = [
            (d, d + step * KV_HEADS)
            for d in range(devices)
            if 0 <= d + step * KV_HEADS < devices
        ]
        return lax.ppermute(x, AXES, pairs)

    def gather_group(own):
        half = own.shape[0] // 2
        one = xor(own, 1)
        four = xor(own, 4)
        five = jnp.concatenate([xor(four[:half], 1), xor(one[half:], 4)], axis=0)
        got = {0: own, 1: one, 4: four, 5: five}
        for k in (0, 1, 4, 5):
            got[k ^ 2] = xor(got[k], 2)
        return [got[k] for k in range(KV_HEADS)]

    def blocks(weight):
        cols = weight.shape[1] // KV_HEADS
        cut = weight.reshape(learner_rows, slices, inner, cols)
        return jnp.transpose(cut, (2, 1, 0, 3)).reshape(KV_HEADS, learner_rows, cols)

    def exchange(stacked):
        groups = [[g * KV_HEADS + j for j in range(KV_HEADS)] for g in range(outer)]
        arrived = lax.all_to_all(
            stacked, AXES, split_axis=0, concat_axis=0, axis_index_groups=groups, tiled=True
        )
        return arrived.reshape(KV_HEADS * learner_rows, stacked.shape[2])

    def gather_line(slab):
        below, above = [], []
        up = down = slab
        for _ in range(outer - 1):
            up = shift(up, 1)
            down = shift(down, -1)
            below.append(up)
            above.append(down)
        every = jnp.stack(below[::-1] + [slab] + above)
        whole = lax.dynamic_slice_in_dim(every, outer - 1 - line, outer, axis=0)
        return whole.reshape(outer * slab.shape[0], slab.shape[1])

    def unswap(parts):
        parts = list(parts)
        bit = 1
        while bit < inner:
            flip = (i & bit) != 0
            parts = [jnp.where(flip, parts[p ^ bit], parts[p]) for p in range(inner)]
            bit *= 2
        return parts

    joined = jnp.concatenate(
        [blocks(query_weight), blocks(key_weight), blocks(value_weight)], axis=2
    )
    weight = gather_line(exchange(joined))
    out_whole = gather_line(exchange(blocks(out_weight)))

    source = hidden_in.astype(jnp.float32)
    squares = jnp.sum(source * source, axis=-1, keepdims=True)
    bit = 1
    while bit < slices:
        squares = squares + xor(squares, bit)
        bit *= 2
    inverse_rms = lax.rsqrt(squares / (features * slices) + epsilon)
    gain = lax.dynamic_slice_in_dim(norm_gain, t * features, features).astype(jnp.float32)
    normed = (source * inverse_rms * gain).astype(jnp.bfloat16)
    tokens = gather_group(normed)
    spans = lax.all_gather(jnp.stack([span_start, span_length]), "fsdp", axis=1, tiled=True)

    bias = jnp.concatenate(
        [
            lax.dynamic_slice_in_dim(query_bias, i * qc, qc),
            lax.dynamic_slice_in_dim(key_bias, i * HEAD, HEAD),
            lax.dynamic_slice_in_dim(value_bias, i * HEAD, HEAD),
        ]
    ).astype(jnp.float32)
    rows = jnp.arange(span_size, dtype=jnp.int32)[:, None]
    columns = jnp.arange(span_size, dtype=jnp.int32)[None, :]
    halves = [
        lax.dynamic_slice_in_dim(weight, (t ^ kt) * features, features) for kt in range(slices)
    ]
    mixes, key_parts, value_parts = [], [], []
    for ki in range(inner):
        projected = bias[None, :]
        for kt in range(slices):
            projected = projected + jnp.dot(
                tokens[ki * slices + kt], halves[kt], preferred_element_type=jnp.float32
            )
        own = lax.dynamic_slice_in_dim(
            spans, (line * inner + (i ^ ki)) * local_spans, local_spans, axis=1
        )
        start, length = own[0], own[1]
        cosine, sine = angles(start, span_size)
        query = rotate(
            projected[:, :qc].reshape(token_rows, GROUPS, HEAD), cosine, sine
        ).astype(jnp.bfloat16)
        keys = rotate(projected[:, None, qc : qc + HEAD], cosine, sine)[:, 0]
        live = (columns < length[:, None]).reshape(token_rows, 1)
        key_cache = jnp.where(live, keys, 0.0).astype(jnp.bfloat16)
        value_cache = jnp.where(live, projected[:, qc + HEAD :], 0.0).astype(jnp.bfloat16)
        query_blocks = query.reshape(local_spans, span_size, GROUPS, HEAD)
        key_blocks = key_cache.reshape(local_spans, span_size, HEAD)
        value_blocks = value_cache.reshape(local_spans, span_size, HEAD)
        scores = jnp.einsum(
            "sqgd,std->sgqt", query_blocks, key_blocks, preferred_element_type=jnp.float32
        ) * HEAD ** (-0.5)
        allowed = (columns <= rows)[None] & (columns[None] < length[:, None, None])
        scores = jnp.where(allowed[:, None], scores, -1e30)
        highest = jnp.max(scores, axis=-1, keepdims=True)
        raised = jnp.exp(scores - highest)
        probs = (raised / jnp.sum(raised, axis=-1, keepdims=True)).astype(jnp.bfloat16)
        mixed = jnp.einsum(
            "sgqt,std->sqgd", probs, value_blocks, preferred_element_type=jnp.float32
        )
        mixes.append(mixed.reshape(token_rows, qc).astype(jnp.bfloat16))
        key_parts.append(key_cache if ki == 0 else xor(key_cache, ki * slices))
        value_parts.append(value_cache if ki == 0 else xor(value_cache, ki * slices))

    mixes = unswap(mixes)
    attended = gather_group(jnp.concatenate(mixes, axis=0))
    combined = 0.0
    for k in range(KV_HEADS):
        head = (t ^ (k % slices)) * inner + (i ^ (k // slices))
        combined = combined + jnp.dot(
            attended[k],
            lax.dynamic_slice_in_dim(out_whole, head * qc, qc),
            preferred_element_type=jnp.float32,
        )
    result = combined.astype(jnp.bfloat16).reshape(inner, token_rows, oc)
    result = unswap([result[p] for p in range(inner)])
    out_parts = [result[0]] + [xor(result[ki], ki * slices) for ki in range(1, inner)]
    return tuple(
        jnp.concatenate(unswap(parts), axis=1)
        for parts in (out_parts, key_parts, value_parts)
    )


def solution(mesh):
    placed = (
        P("fsdp", "tensor"),
        P(),
        P(("fsdp", "tensor"), None),
        P(("fsdp", "tensor"), None),
        P(("fsdp", "tensor"), None),
        P(("fsdp", "tensor"), None),
        P("tensor"),
        P("tensor"),
        P("tensor"),
        P("fsdp"),
        P("fsdp"),
    )
    return jax.shard_map(
        local,
        mesh=mesh,
        in_specs=placed,
        out_specs=(P("fsdp", "tensor"), P("fsdp", "tensor"), P("fsdp", "tensor")),
        check_vma=False,
    )
```

time: 1490 us -> 645 us (0.43)
  waiting for transfers between devices: 1280 us -> 228 us
  blocking collectives: 0 us -> 85.9 us
  matrix products: 53.5 us -> 121 us
  local copies, waits for them, and re-layouts: 63.8 us -> 112 us
  starting transfers between devices: 30.4 us -> 58.9 us
    all_to_all x2 -> x1, waiting for transfers between devices: 1070 us -> 0.01 us  [exchange(): lax.all_to_all(stacked, AXES, split_axis=0, concat_axis=0, axis_index_gro...]
    ppermute x0 -> x38, waiting for transfers between devices: none -> 228 us  [the longest x12 116 us: shift(): return lax.ppermute(x, AXES, pairs)]
    all_gather x2 -> x0, waiting for transfers between devices: 213 us -> none  [the longest x1 213 us: local(): gathered = lax.all_gather(hidden_in, 'tensor', axis=1, tiled=True)]
    ppermute x0 -> x38, starting transfers between devices: none -> 55.3 us  [the longest x12 37.1 us: shift(): return lax.ppermute(x, AXES, pairs)]
    all_gather x0 -> x1, blocking collectives: none -> 52.8 us  [local(): lax.all_gather(jnp.stack([span_start, span_length]), 'fsdp', axis=1, tile...]
    dot_general x4 -> x20, matrix products: 53.5 us -> 104 us  [the longest x8 56.5 us: local(): jnp.dot(attended[k], lax.dynamic_slice_in_dim(out_whole, head * qc, qc),...]
    unnamed x20 -> x102, local copies, waits for them, and re-layouts: 5.2 us -> 41.3 us
    all_to_all x0 -> x1, blocking collectives: none -> 33.1 us  [exchange(): lax.all_to_all(stacked, AXES, split_axis=0, concat_axis=0, axis_index_gro...]
  transfers between devices with their start and end apart: 4 -> 39, of which waited for: 3 -> 13; matrix products, arithmetic and copies ran while one was open for 7% -> 37% of each run, Pallas kernels for 0% -> 0%
where the time goes in v1:
time: 645 us; the launch traced here: 636 us
  waiting for transfers between devices  228 us (35%)
  matrix products  121 us (19%)
  local copies, waits for them, and re-layouts  112 us (17%)
  blocking collectives  85.9 us (13%)
  starting transfers between devices  58.9 us (9%)
  other arithmetic  27.9 us (4%)
    ppermute x12, waiting for transfers between devices, shift(): return lax.ppermute(x, AXES, pairs)  116 us
    ppermute x26, waiting for transfers between devices, xor(): return lax.ppermute(x, AXES, [(d, d ^ k) for d in range(devices)])  112 us
    dot_general x8, matrix products, local(): jnp.dot(attended[k], lax.dynamic_slice_in_dim(out_whole, head * qc, qc),...  56.5 us
    all_gather x1, blocking collectives, local(): lax.all_gather(jnp.stack([span_start, span_length]), 'fsdp', axis=1, tile...  52.8 us
    unnamed x102, local copies, waits for them, and re-layouts  41.3 us
    ppermute x12, starting transfers between devices, shift(): return lax.ppermute(x, AXES, pairs)  37.1 us
    dot_general x8, matrix products, local(): jnp.dot(tokens[ki * slices + kt], halves[kt], preferred_element_type=jnp....  36 us
    all_to_all x1, blocking collectives, exchange(): lax.all_to_all(stacked, AXES, split_axis=0, concat_axis=0, axis_index_gro...  33.1 us
  transfers between devices with their start and end apart: 39, of which 13 were waited for; matrix products, arithmetic and copies ran while one was open for 37% of the time, Pallas kernels for 0%

profile of v1, /device:TPU:0, one launch (start us, length us, event | category | flops | bytes accessed | tf_op | source)
XLA Modules:
  0.0 635.6 jit_solution(2110706258511932492)
XLA Ops:
  6.9 33.1 %all_to_all.10 = bf16[8,160,896]{2,1,0:T(8,128)(2,1)} all-to-all(bf16[8,160,896]{2,1,0:T(8,128)(2,1)S(1)} %pad_maximum_fusion.1), channel_id=1, replica_groups={{0,1,2,3,4,5,6,7},{8,9,10,11,12,13,14,15},{16,17,18,19,20,21,22,23},{24..., dimensions={0} | all-to-all | bytes 4587520 | tf_op jit(solution)/shard_map/all_to_all | solution.py:88
  54.0 39.6 %collective-permute-done.3 = bf16[1280,896]{1,0:T(8,128)(2,1)} collective-permute-done((bf16[1280,896]{1,0:T(8,128)(2,1)}, bf16[1280,896]{1,0:T(8,128)(2,1)}, u32[]{:S(2)}, u32[]{:S(2)}) %collective-permute-start.3) | collective-permute-done | bytes 2293792 | tf_op jit(solution)/shard_map/ppermute | solution.py:69
  93.6 5.7 collective-permute-start.4
  109.7 52.8 %all-gather = s32[16,2,2]{2,1,0:T(2,128)S(1)} all-gather(s32[1,2,2]{2,1,0:T(2,128)S(1)} %bitcast.327), channel_id=1, replica_groups=mesh['fsdp'=16,'tensor'=2] {'fsdp'}, dimensions={0}, use_global_device_ids=true | all-gather | bytes 272 | tf_op jit(solution)/shard_map/all_gather | solution.py:130
  164.5 6.0 collective-permute-start.5
  173.2 11.9 %collective-permute-done.10 = bf16[512,2560]{1,0:T(8,128)(2,1)} collective-permute-done((bf16[512,2560]{1,0:T(8,128)(2,1)}, bf16[512,2560]{1,0:T(8,128)(2,1)}, u32[]{:S(2)}, u32[]{:S(2)}) %collective-permute-start.10) | collective-permute-done | bytes 2621472 | tf_op jit(solution)/shard_map/ppermute | solution.py:61
  194.6 17.9 %collective-permute-done.9 = bf16[256,2560]{1,0:T(8,128)(2,1)S(1)} collective-permute-done((bf16[256,2560]{1,0:T(8,128)(2,1)}, bf16[256,2560]{1,0:T(8,128)(2,1)S(1)}, u32[]{:S(2)}, u32[]{:S(2)}) %collective-permute-start.9) | collective-permute-done | bytes 1310752 | tf_op jit(solution)/shard_map/ppermute | solution.py:61
  242.7 10.9 %collective-permute-done.15 = bf16[1280,640]{1,0:T(8,128)(2,1)} collective-permute-done((bf16[1280,640]{1,0:T(8,128)(2,1)S(1)}, bf16[1280,640]{1,0:T(8,128)(2,1)}, u32[]{:S(2)}, u32[]{:S(2)}) %collective-permute-start.15) | collective-permute-done | bytes 1638432 | tf_op jit(solution)/shard_map/ppermute | solution.py:69
  253.6 51.4 %collective-permute-done.8 = bf16[1280,896]{1,0:T(8,128)(2,1)S(1)} collective-permute-done((bf16[1280,896]{1,0:T(8,128)(2,1)}, bf16[1280,896]{1,0:T(8,128)(2,1)S(1)}, u32[]{:S(2)}, u32[]{:S(2)}) %collective-permute-start.8) | collective-permute-done | bytes 2293792 | tf_op jit(solution)/shard_map/ppermute | solution.py:69
  310.1 7.9 %constant_dynamic-slice_fusion.4 = bf16[4,1280,896]{2,1,0:T(8,128)(2,1)} fusion(bf16[7,1280,896]{2,1,0:T(8,128)(2,1)} %bitcast_dynamic-update-slice_fusion, s32[]{:T(128)S(6)} %select_n.333), kind=kLoop, calls=%fused_computation.265 | loop fusion | bytes 18350084 | tf_op jit(solution)/shard_map/dynamic_slice | solution.py:102
  318.0 6.1 fusion.17
  348.0 5.7 fusion.19
  426.9 5.7 collective-permute-start.17
  450.9 14.3 %collective-permute-done.19 = bf16[1280,640]{1,0:T(8,128)(2,1)S(1)} collective-permute-done((bf16[1280,640]{1,0:T(8,128)(2,1)}, bf16[1280,640]{1,0:T(8,128)(2,1)S(1)}, u32[]{:S(2)}, u32[]{:S(2)}) %collective-permute-start.19) | collective-permute-done | bytes 1638432 | tf_op jit(solution)/shard_map/ppermute | solution.py:69
  476.3 31.1 %collective-permute-done.24 = bf16[2048,640]{0,1:T(8,128)(2,1)} collective-permute-done((bf16[2048,640]{0,1:T(8,128)(2,1)}, bf16[2048,640]{0,1:T(8,128)(2,1)}, u32[]{:S(2)}, u32[]{:S(2)}) %collective-permute-start.24) | collective-permute-done | bytes 2621472 | tf_op jit(solution)/shard_map/ppermute | solution.py:61
  518.5 19.6 %collective-permute-done.25 = bf16[1024,640]{0,1:T(8,128)(2,1)S(1)} collective-permute-done((bf16[1024,640]{0,1:T(8,128)(2,1)S(1)}, bf16[1024,640]{0,1:T(8,128)(2,1)S(1)}, u32[]{:S(2)}, u32[]{:S(2)}) %collective-permute-start.25) | collective-permute-done | bytes 1310752 | tf_op jit(solution)/shard_map/ppermute | solution.py:61
  544.0 8.1 %fusion.58 = f32[2048,640]{0,1:T(8,128)} fusion(bf16[2048,640]{0,1:T(8,128)(2,1)} %constant_dynamic-update-slice_fusion.2, bf16[5120,640]{1,0:T(8,128)(2,1)S(1)} %bitcast.279, s32[]{:T(128)S(6)} %select_n.366), kind=kOutput, calls=%fused_computation.91 | convolution fusion | flops 1677721600 | bytes 8683524 | tf_op jit(solution)/shard_map/dot_general | solution.py:186
  552.1 6.3 fusion.56
  558.4 6.3 fusion.50
  574.2 6.4 %fusion.52 = f32[2048,640]{0,1:T(8,128)} fusion(bf16[2048,640]{0,1:T(8,128)(2,1)} %collective-permute-done.23, bf16[5120,640]{1,0:T(8,128)(2,1)S(1)} %bitcast.284, s32[]{:T(128)S(6)} %select_n.369), kind=kOutput, calls=%fused_computation.85 | convolution fusion | flops 1677721600 | bytes 8683524 | tf_op jit(solution)/shard_map/dot_general | solution.py:186
  580.6 6.3 fusion.45
  586.9 13.6 %add_convert_fusion = bf16[2048,640]{0,1:T(8,128)(2,1)S(1)} fusion(f32[2048,640]{0,1:T(8,128)} %fusion.45, f32[2048,640]{0,1:T(8,128)} %fusion.48, f32[2048,640]{0,1:T(8,128)} %fusion.50, f32[2048,640]{0,1:T(8,128)} %fusion.52, f32[2048,640]{0,1:T(8,128)} %fusion.54, f32[2048,640]{0,1:T(8,128)} %fusion.58, f32[2048,640]{0,1:T(8,128)} %fusion.56, ...), kind=kOutput, calls=%fused_computation.9 | convolution fusion | flops 1688207360 | bytes 42762244 | tf_op jit(solution)/shard_map/dot_general | solution.py:186
  605.7 11.9 %collective-permute-done.29 = bf16[512,640]{0,1:T(8,128)(2,1)S(1)} collective-permute-done((bf16[512,640]{0,1:T(8,128)(2,1)S(1)}, bf16[512,640]{0,1:T(8,128)(2,1)S(1)}, u32[]{:S(2)}, u32[]{:S(2)}) %collective-permute-start.29) | collective-permute-done | bytes 655392 | tf_op jit(solution)/shard_map/ppermute | solution.py:61
  617.6 14.4 %collective-permute-done.30 = bf16[512,640]{0,1:T(8,128)(2,1)S(1)} collective-permute-done((bf16[512,640]{0,1:T(8,128)(2,1)S(1)}, bf16[512,640]{0,1:T(8,128)(2,1)S(1)}, u32[]{:S(2)}, u32[]{:S(2)}) %collective-permute-start.30) | collective-permute-done | bytes 655392 | tf_op jit(solution)/shard_map/ppermute | solution.py:61
  (278 shorter events, 240.7 us)
Async XLA Ops:
  40.1 53.5 %collective-permute-start.3 = (bf16[1280,896]{1,0:T(8,128)(2,1)}, bf16[1280,896]{1,0:T(8,128)(2,1)}, u32[]{:S(2)}, u32[]{:S(2)}) collective-permute-start(bf16[1280,896]{1,0:T(8,128)(2,1)} %bitcast.15), channel_id=1, source_target_pairs={{0,8},{1,9},{2,10},{3,11},{4,12},{5,13},{6,14},{7,15},{8,16},{9,17... | collective-permute-start | bytes 6881288 | tf_op jit(solution)/shard_map/ppermute | solution.py:69
  51.4 119.1 %collective-permute-start.1 = (bf16[512,2560]{1,0:T(8,128)(2,1)}, bf16[512,2560]{1,0:T(8,128)(2,1)}, u32[]{:S(2)}, u32[]{:S(2)}) collective-permute-start(bf16[512,2560]{1,0:T(8,128)(2,1)} %fusion.6), channel_id=1, source_target_pairs={{0,4},{1,5},{2,6},{3,7},{4,0},{5,1},{6,2},{7,3},{8,12},{9,13},{10,... | collective-permute-start | bytes 7864328 | tf_op jit(solution)/shard_map/ppermute | solution.py:61
  52.7 110.5 %collective-permute-start.6 = (bf16[1280,896]{1,0:T(8,128)(2,1)}, bf16[1280,896]{1,0:T(8,128)(2,1)}, u32[]{:S(2)}, u32[]{:S(2)}) collective-permute-start(bf16[1280,896]{1,0:T(8,128)(2,1)} %bitcast.15), channel_id=1, source_target_pairs={{8,0},{9,1},{10,2},{11,3},{12,4},{13,5},{14,6},{15,7},{16,8},{17,9... | collective-permute-start | bytes 6881288 | tf_op jit(solution)/shard_map/ppermute | solution.py:69
  93.6 70.9 %collective-permute-start.4 = (bf16[1280,896]{1,0:T(8,128)(2,1)}, bf16[1280,896]{1,0:T(8,128)(2,1)}, u32[]{:S(2)}, u32[]{:S(2)}) collective-permute-start(bf16[1280,896]{1,0:T(8,128)(2,1)} %collective-permute-done.3), channel_id=1, source_target_pairs={{0,8},{1,9},{2,10},{3,11},{4,12},{5,13},{6,14},{7,15},{8,16},{9,17... | collective-permute-start | bytes 6881288 | tf_op jit(solution)/shard_map/ppermute | solution.py:69
  104.0 90.6 %all-to-all-start.1 = ((bf16[8,160,640]{2,1,0:T(8,128)(2,1)}), bf16[8,160,640]{2,1,0:T(8,128)(2,1)S(1)}, u32[]{:S(2)}, u32[]{:S(2)}) async-start(bf16[8,160,640]{2,1,0:T(8,128)(2,1)} %bitcast.71), calls=%async_computation.1 | async-start | bytes 3276800 | tf_op jit(solution)/shard_map/all_to_all | solution.py:88
  107.6 77.4 %collective-permute-start.10 = (bf16[512,2560]{1,0:T(8,128)(2,1)}, bf16[512,2560]{1,0:T(8,128)(2,1)}, u32[]{:S(2)}, u32[]{:S(2)}) collective-permute-start(bf16[512,2560]{1,0:T(8,128)(2,1)} %fusion.6), channel_id=1, source_target_pairs={{0,1},{1,0},{2,3},{3,2},{4,5},{5,4},{6,7},{7,6},{8,9},{9,8},{10,11... | collective-permute-start | bytes 7864328 | tf_op jit(solution)/shard_map/ppermute | solution.py:61
  163.2 57.4 %collective-permute-start.7 = (bf16[1280,896]{1,0:T(8,128)(2,1)}, bf16[1280,896]{1,0:T(8,128)(2,1)}, u32[]{:S(2)}, u32[]{:S(2)}) collective-permute-start(bf16[1280,896]{1,0:T(8,128)(2,1)} %collective-permute-done.6), channel_id=1, source_target_pairs={{8,0},{9,1},{10,2},{11,3},{12,4},{13,5},{14,6},{15,7},{16,8},{17,9... | collective-permute-start | bytes 6881288 | tf_op jit(solution)/shard_map/ppermute | solution.py:69
  164.5 57.6 %collective-permute-start.5 = (bf16[1280,896]{1,0:T(8,128)(2,1)}, bf16[1280,896]{1,0:T(8,128)(2,1)}, u32[]{:S(2)}, u32[]{:S(2)}) collective-permute-start(bf16[1280,896]{1,0:T(8,128)(2,1)} %collective-permute-done.4), channel_id=1, source_target_pairs={{0,8},{1,9},{2,10},{3,11},{4,12},{5,13},{6,14},{7,15},{8,16},{9,17... | collective-permute-start | bytes 6881288 | tf_op jit(solution)/shard_map/ppermute | solution.py:69
  194.6 123.4 %collective-permute-start.13 = (bf16[512,2560]{1,0:T(8,128)(2,1)}, bf16[512,2560]{1,0:T(8,128)(2,1)}, u32[]{:S(2)}, u32[]{:S(2)}) collective-permute-start(bf16[512,2560]{1,0:T(8,128)(2,1)} %fusion.6), channel_id=1, source_target_pairs={{0,2},{1,3},{2,0},{3,1},{4,6},{5,7},{6,4},{7,5},{8,10},{9,11},{10,... | collective-permute-start | bytes 7864328 | tf_op jit(solution)/shard_map/ppermute | solution.py:61
  212.6 41.1 %collective-permute-start.15 = (bf16[1280,640]{1,0:T(8,128)(2,1)S(1)}, bf16[1280,640]{1,0:T(8,128)(2,1)}, u32[]{:S(2)}, u32[]{:S(2)}) collective-permute-start(bf16[1280,640]{1,0:T(8,128)(2,1)S(1)} %bitcast.287), channel_id=1, source_target_pairs={{0,8},{1,9},{2,10},{3,11},{4,12},{5,13},{6,14},{7,15},{8,16},{9,17... | collective-permute-start | bytes 4915208 | tf_op jit(solution)/shard_map/ppermute | solution.py:69
  217.8 199.7 %collective-permute-start.18 = (bf16[1280,640]{1,0:T(8,128)(2,1)S(1)}, bf16[1280,640]{1,0:T(8,128)(2,1)}, u32[]{:S(2)}, u32[]{:S(2)}) collective-permute-start(bf16[1280,640]{1,0:T(8,128)(2,1)S(1)} %bitcast.288), channel_id=1, source_target_pairs={{8,0},{9,1},{10,2},{11,3},{12,4},{13,5},{14,6},{15,7},{16,8},{17,9... | collective-permute-start | bytes 4915208 | tf_op jit(solution)/shard_map/ppermute | solution.py:69
  220.6 103.6 %collective-permute-start.14 = (bf16[512,2560]{1,0:T(8,128)(2,1)}, bf16[512,2560]{1,0:T(8,128)(2,1)}, u32[]{:S(2)}, u32[]{:S(2)}) collective-permute-start(bf16[512,2560]{1,0:T(8,128)(2,1)} %collective-permute-done.10), channel_id=1, source_target_pairs={{0,2},{1,3},{2,0},{3,1},{4,6},{5,7},{6,4},{7,5},{8,10},{9,11},{10,... | collective-permute-start | bytes 7864328 | tf_op jit(solution)/shard_map/ppermute | solution.py:61
  222.0 83.0 %collective-permute-start.8 = (bf16[1280,896]{1,0:T(8,128)(2,1)}, bf16[1280,896]{1,0:T(8,128)(2,1)S(1)}, u32[]{:S(2)}, u32[]{:S(2)}) collective-permute-start(bf16[1280,896]{1,0:T(8,128)(2,1)} %collective-permute-done.7), channel_id=1, source_target_pairs={{8,0},{9,1},{10,2},{11,3},{12,4},{13,5},{14,6},{15,7},{16,8},{17,9... | collective-permute-start | bytes 6881288 | tf_op jit(solution)/shard_map/ppermute | solution.py:69
  253.6 89.7 %collective-permute-start.2 = (bf16[512,2560]{1,0:T(8,128)(2,1)}, bf16[512,2560]{1,0:T(8,128)(2,1)}, u32[]{:S(2)}, u32[]{:S(2)}) collective-permute-start(bf16[512,2560]{1,0:T(8,128)(2,1)} %collective-permute-done.1), channel_id=1, source_target_pairs={{0,2},{1,3},{2,0},{3,1},{4,6},{5,7},{6,4},{7,5},{8,10},{9,11},{10,... | collective-permute-start | bytes 7864328 | tf_op jit(solution)/shard_map/ppermute | solution.py:61
  305.0 112.6 %collective-permute-start.16 = (bf16[1280,640]{1,0:T(8,128)(2,1)}, bf16[1280,640]{1,0:T(8,128)(2,1)}, u32[]{:S(2)}, u32[]{:S(2)}) collective-permute-start(bf16[1280,640]{1,0:T(8,128)(2,1)} %collective-permute-done.15), channel_id=1, source_target_pairs={{0,8},{1,9},{2,10},{3,11},{4,12},{5,13},{6,14},{7,15},{8,16},{9,17... | collective-permute-start | bytes 4915208 | tf_op jit(solution)/shard_map/ppermute | solution.py:69
  362.8 56.4 %collective-permute-start.34 = (bf16[512,128]{1,0:T(8,128)(2,1)}, bf16[512,128]{1,0:T(8,128)(2,1)}, u32[]{:S(2)}, u32[]{:S(2)}) collective-permute-start(bf16[512,128]{1,0:T(8,128)(2,1)} %get-tuple-element.20), channel_id=1, source_target_pairs={{0,2},{1,3},{2,0},{3,1},{4,6},{5,7},{6,4},{7,5},{8,10},{9,11},{10,... | collective-permute-start | bytes 393224 | tf_op jit(solution)/shard_map/ppermute | solution.py:61
  363.3 62.2 %collective-permute-start.37 = (bf16[512,128]{1,0:T(8,128)(2,1)}, bf16[512,128]{1,0:T(8,128)(2,1)}, u32[]{:S(2)}, u32[]{:S(2)}) collective-permute-start(bf16[512,128]{1,0:T(8,128)(2,1)} %get-tuple-element.97), channel_id=1, source_target_pairs={{0,2},{1,3},{2,0},{3,1},{4,6},{5,7},{6,4},{7,5},{8,10},{9,11},{10,... | collective-permute-start | bytes 393224 | tf_op jit(solution)/shard_map/ppermute | solution.py:61
  365.5 67.1 %collective-permute-start.35 = (bf16[512,128]{1,0:T(8,128)(2,1)}, bf16[512,128]{1,0:T(8,128)(2,1)}, u32[]{:S(2)}, u32[]{:S(2)}) collective-permute-start(bf16[512,128]{1,0:T(8,128)(2,1)} %get-tuple-element.99), channel_id=1, source_target_pairs={{0,6},{1,7},{2,4},{3,5},{4,2},{5,3},{6,0},{7,1},{8,14},{9,15},{10,... | collective-permute-start | bytes 393224 | tf_op jit(solution)/shard_map/ppermute | solution.py:61
  449.0 58.5 %collective-permute-start.24 = (bf16[2048,640]{0,1:T(8,128)(2,1)}, bf16[2048,640]{0,1:T(8,128)(2,1)}, u32[]{:S(2)}, u32[]{:S(2)}) collective-permute-start(bf16[2048,640]{0,1:T(8,128)(2,1)} %constant_dynamic-update-slice_fusion.2), channel_id=1, source_target_pairs={{0,4},{1,5},{2,6},{3,7},{4,0},{5,1},{6,2},{7,3},{8,12},{9,13},{10,... | collective-permute-start | bytes 7864328 | tf_op jit(solution)/shard_map/ppermute | solution.py:61
  450.6 58.8 %collective-permute-start.21 = (bf16[2048,640]{0,1:T(8,128)(2,1)}, bf16[2048,640]{0,1:T(8,128)(2,1)}, u32[]{:S(2)}, u32[]{:S(2)}) collective-permute-start(bf16[2048,640]{0,1:T(8,128)(2,1)} %constant_dynamic-update-slice_fusion.2), channel_id=1, source_target_pairs={{0,1},{1,0},{2,3},{3,2},{4,5},{5,4},{6,7},{7,6},{8,9},{9,8},{10,11... | collective-permute-start | bytes 7864328 | tf_op jit(solution)/shard_map/ppermute | solution.py:61
  465.2 51.5 %collective-permute-start.20 = (bf16[1280,640]{1,0:T(8,128)(2,1)S(1)}, bf16[1280,640]{1,0:T(8,128)(2,1)S(1)}, u32[]{:S(2)}, u32[]{:S(2)}) collective-permute-start(bf16[1280,640]{1,0:T(8,128)(2,1)S(1)} %collective-permute-done.19), channel_id=1, source_target_pairs={{8,0},{9,1},{10,2},{11,3},{12,4},{13,5},{14,6},{15,7},{16,8},{17,9... | collective-permute-start | bytes 4915208 | tf_op jit(solution)/shard_map/ppermute | solution.py:69
  516.6 48.0 %collective-permute-start.22 = (bf16[2048,640]{0,1:T(8,128)(2,1)}, bf16[2048,640]{0,1:T(8,128)(2,1)S(1)}, u32[]{:S(2)}, u32[]{:S(2)}) collective-permute-start(bf16[2048,640]{0,1:T(8,128)(2,1)} %constant_dynamic-update-slice_fusion.2), channel_id=1, source_target_pairs={{0,2},{1,3},{2,0},{3,1},{4,6},{5,7},{6,4},{7,5},{8,10},{9,11},{10,... | collective-permute-start | bytes 7864328 | tf_op jit(solution)/shard_map/ppermute | solution.py:61
  518.0 56.3 %collective-permute-start.23 = (bf16[2048,640]{0,1:T(8,128)(2,1)}, bf16[2048,640]{0,1:T(8,128)(2,1)}, u32[]{:S(2)}, u32[]{:S(2)}) collective-permute-start(bf16[2048,640]{0,1:T(8,128)(2,1)} %collective-permute-done.21), channel_id=1, source_target_pairs={{0,2},{1,3},{2,0},{3,1},{4,6},{5,7},{6,4},{7,5},{8,10},{9,11},{10,... | collective-permute-start | bytes 7864328 | tf_op jit(solution)/shard_map/ppermute | solution.py:61
  543.4 43.5 %collective-permute-start.27 = (bf16[2048,640]{0,1:T(8,128)(2,1)}, bf16[2048,640]{0,1:T(8,128)(2,1)S(1)}, u32[]{:S(2)}, u32[]{:S(2)}) collective-permute-start(bf16[2048,640]{0,1:T(8,128)(2,1)} %collective-permute-done.24), channel_id=1, source_target_pairs={{0,2},{1,3},{2,0},{3,1},{4,6},{5,7},{6,4},{7,5},{8,10},{9,11},{10,... | collective-permute-start | bytes 7864328 | tf_op jit(solution)/shard_map/ppermute | solution.py:61
  (51 other events, 695.9 us)

commit v2 on v1

--- a/solution.py
+++ b/solution.py
@@ -1,6 +1,10 @@
+import functools
+
 import jax
 import jax.numpy as jnp
 from jax import lax
+from jax.experimental import pallas as pl
+from jax.experimental.pallas import tpu as pltpu
 from jax.sharding import PartitionSpec as P
 
 HEADS = 40
@@ -27,6 +31,418 @@
     inverse = 1.0 / rope_base ** (jnp.arange(0, HEAD, 2, dtype=jnp.float32) / HEAD)
     phase = positions.reshape(-1).astype(jnp.float32)[:, None] * inverse[None, :]
     return (jnp.cos(phase)[:, None, :], jnp.sin(phase)[:, None, :])
+
+
+MESH = pl.DeviceIdType.MESH
+G = KV_HEADS
+QC = GROUPS * HEAD
+
+
+def flip(m, bit):
+    return m + bit - 2 * bit * (lax.div(m, bit) % 2)
+
+
+def body(
+    members, slices, spans, span_size,
+    normed, joined, outs, bias, cosine, sine, length,
+    out, key_out, value_out, gathered,
+    wq, wo, tokens, own, keys, values, result, buffer,
+    a_send, a_recv, a_own, b_send, b_recv, b_own,
+    zq_send, zq_recv, zo_send, zo_recv,
+    t_send, t_recv, t_own, g_send, g_recv, g_own,
+    load, r_send, r_recv, k_send, k_recv, v_send, v_recv,
+):
+    inner = G // slices
+    line_size = members // inner
+    f = lax.axis_index("fsdp")
+    t = lax.axis_index("tensor")
+    o = lax.div(f, inner)
+    i = f % inner
+    me = i * slices + t
+    rows = joined.shape[1]
+    mx, my, mc = flip(me, 4), flip(me, 1), flip(me, 2)
+    md = flip(mx, 1)
+
+    def member(m):
+        return (o * inner + lax.div(m, slices), m % slices)
+
+    def remote(src, dst, ss, rs, where):
+        return pltpu.make_async_remote_copy(
+            src_ref=src, dst_ref=dst, send_sem=ss, recv_sem=rs, device_id=where, device_id_type=MESH
+        )
+
+    barrier = pltpu.get_barrier_semaphore()
+    for d in range(1, G):
+        pl.semaphore_signal(
+            barrier, inc=1, device_id=member((me + d) % G), device_id_type=MESH
+        )
+
+    @pl.when(o > 0)
+    def _():
+        pl.semaphore_signal(barrier, inc=1, device_id=(f - inner, t), device_id_type=MESH)
+
+    @pl.when(o < line_size - 1)
+    def _():
+        pl.semaphore_signal(barrier, inc=1, device_id=(f + inner, t), device_id_type=MESH)
+
+    ends = (o == 0).astype(jnp.int32) + (o == line_size - 1).astype(jnp.int32)
+    pl.semaphore_wait(barrier, G + 1 - ends)
+
+    def place(buf, origin, m, count):
+        return buf.at[pl.ds(pl.multiple_of((origin * G + m) * rows, rows), count * rows), :]
+
+    def trade(src, buf, ss, rs, d):
+        to = (me + d) % G
+        return remote(src.at[to], place(buf, o, me, 1), ss.at[d], rs.at[d], member(to))
+
+    def trade_own(src, buf, sem):
+        return pltpu.make_async_copy(src.at[me], place(buf, o, me, 1), sem)
+
+    def trade_start(src, buf, ss, rs, sem):
+        trade_own(src, buf, sem).start()
+        for d in range(1, G):
+            trade(src, buf, ss, rs, d).start()
+
+    def trade_wait(src, buf, ss, rs, sem, m):
+        @pl.when(m == me)
+        def _():
+            trade_own(src, buf, sem).wait()
+
+        @pl.when(m != me)
+        def _():
+            d = (me - m + G) % G
+            here = place(buf, o, m, 1)
+            remote(here, here, ss.at[d], rs.at[d], member(m)).wait_recv()
+
+    def hop(buf, ss, rs, origin, c, way):
+        here = place(buf, origin, 2 * c, 2)
+        way_f = f + inner if way == 0 else f - inner
+        return remote(here, here, ss.at[way, origin, c], rs.at[origin, c], (way_f, t))
+
+    def forward(buf, ss, rs, s, c):
+        below, above = o - s, o + s
+        if s > 0:
+            @pl.when(below >= 0)
+            def _():
+                hop(buf, ss, rs, below, c, 0).wait_recv()
+
+            @pl.when(above < line_size)
+            def _():
+                hop(buf, ss, rs, above, c, 0).wait_recv()
+
+        @pl.when(jnp.logical_and(below >= 0, o < line_size - 1))
+        def _():
+            hop(buf, ss, rs, below, c, 0).start()
+
+        @pl.when(jnp.logical_and(above < line_size, o > 0))
+        def _():
+            hop(buf, ss, rs, above, c, 1).start()
+
+    def hops_sent(buf, ss, rs):
+        for s in range(line_size):
+            for c in range(G // 2):
+                below, above = o - s, o + s
+
+                @pl.when(jnp.logical_and(below >= 0, o < line_size - 1))
+                def _():
+                    hop(buf, ss, rs, below, c, 0).wait_send()
+
+                @pl.when(jnp.logical_and(above < line_size, o > 0))
+                def _():
+                    hop(buf, ss, rs, above, c, 1).wait_send()
+
+    def piece(buf, m, n):
+        return buf.at[m, pl.ds(pl.multiple_of(n * span_size, span_size), span_size), :]
+
+    def mine(src, n):
+        return src.at[pl.ds(pl.multiple_of(n * span_size, span_size), span_size), :]
+
+    def send_own(src, buf, ss, rs, sem, n):
+        for kind, to in ((0, mx), (1, my), (2, mc)):
+            remote(
+                mine(src, n), piece(buf, me, n), ss.at[kind, n], rs.at[kind, n], member(to)
+            ).start()
+        pltpu.make_async_copy(mine(src, n), piece(buf, me, n), sem.at[n]).start()
+
+    def arrived(buf, ss, rs, kind, slot, n):
+        here = piece(buf, slot, n)
+        remote(here, here, ss.at[kind, n], rs.at[kind, n], member(mx)).wait_recv()
+
+    def pass_on(buf, ss, rs, kind, slot, to, n):
+        here = piece(buf, slot, n)
+        remote(here, here, ss.at[kind, n], rs.at[kind, n], member(to)).start()
+
+    def relay(buf, ss, rs, n, total):
+        arrived(buf, ss, rs, 0, mx, n)
+        arrived(buf, ss, rs, 1, my, n)
+
+        @pl.when(n < total // 2)
+        def _():
+            pass_on(buf, ss, rs, 3, mx, my, n)
+
+        @pl.when(n >= total // 2)
+        def _():
+            pass_on(buf, ss, rs, 3, my, mx, n)
+
+        pass_on(buf, ss, rs, 4, mx, mc, n)
+        pass_on(buf, ss, rs, 5, my, mc, n)
+
+    def relay_far(buf, ss, rs, n):
+        arrived(buf, ss, rs, 3, md, n)
+        pass_on(buf, ss, rs, 6, md, mc, n)
+
+    def settle(src, buf, ss, rs, sem, n):
+        pltpu.make_async_copy(mine(src, n), piece(buf, me, n), sem.at[n]).wait()
+        for kind, slot in ((2, mc), (4, flip(mx, 2)), (5, flip(my, 2)), (6, flip(md, 2))):
+            arrived(buf, ss, rs, kind, slot, n)
+
+    def sent(buf, ss, rs, n):
+        for kind in range(7):
+            here = piece(buf, me, n)
+            remote(here, here, ss.at[kind, n], rs.at[kind, n], member(mx)).wait_send()
+
+    trade_start(joined, wq, a_send, a_recv, a_own)
+    for n in range(spans):
+        send_own(normed, tokens, t_send, t_recv, t_own, n)
+    for c in range(G // 2):
+        for m in (2 * c, 2 * c + 1):
+            trade_wait(joined, wq, a_send, a_recv, a_own, m)
+        forward(wq, zq_send, zq_recv, 0, c)
+    for n in range(spans):
+        relay(tokens, t_send, t_recv, n, spans)
+    for c in range(G // 2):
+        forward(wq, zq_send, zq_recv, 1, c)
+    trade_start(outs, wo, b_send, b_recv, b_own)
+    for n in range(spans):
+        relay_far(tokens, t_send, t_recv, n)
+    for s in range(2, line_size):
+        if s == line_size - 1:
+            for c in range(G // 2):
+                for m in (2 * c, 2 * c + 1):
+                    trade_wait(outs, wo, b_send, b_recv, b_own, m)
+                forward(wo, zo_send, zo_recv, 0, c)
+        for c in range(G // 2):
+            forward(wq, zq_send, zq_recv, s, c)
+    for n in range(spans):
+        settle(normed, tokens, t_send, t_recv, t_own, n)
+
+    pieces = inner * spans
+    features = tokens.shape[2]
+    scale = HEAD ** (-0.5)
+
+    def chunk_copy(stage, target, ss, rs, p):
+        src = stage.at[pl.ds(pl.multiple_of(p * spans * span_size, span_size), spans * span_size), :]
+        dst = target.at[:, pl.ds(pl.multiple_of(i * HEAD, HEAD), HEAD)]
+        return (
+            pltpu.make_async_copy(src, dst, ss.at[p]),
+            remote(src, dst, ss.at[p], rs.at[i], (o * inner + p, t)),
+        )
+
+    def chunk_arrived(stage, target, ss, rs, p):
+        src = stage.at[pl.ds(0, spans * span_size), :]
+        dst = target.at[:, pl.ds(pl.multiple_of(p * HEAD, HEAD), HEAD)]
+        remote(src, dst, ss.at[p], rs.at[p], (o * inner + p, t)).wait_recv()
+
+    def one_span(n, carry):
+        p = lax.div(n, spans)
+        part = n % spans
+        here = pl.ds(pl.multiple_of(n * span_size, span_size), span_size)
+        projected = bias[...]
+        for half in range(slices):
+            projected = projected + jnp.dot(
+                tokens[p * slices + half, pl.ds(pl.multiple_of(part * span_size, span_size), span_size), :],
+                wq[pl.ds(half * features, features), :],
+                preferred_element_type=jnp.float32,
+            )
+        cos, sin = cosine[here, :], sine[here, :]
+
+        def turn(x):
+            return x * cos + pltpu.roll(x, HEAD // 2, 1) * sin
+
+        size = length[n]
+        live = lax.broadcasted_iota(jnp.int32, (span_size, HEAD), 0) < size
+        key = jnp.where(live, turn(projected[:, QC : QC + HEAD]), 0.0).astype(jnp.bfloat16)
+        value = jnp.where(live, projected[:, QC + HEAD :], 0.0).astype(jnp.bfloat16)
+        keys[here, :] = key
+        values[here, :] = value
+        row = lax.broadcasted_iota(jnp.int32, (span_size, span_size), 0)
+        column = lax.broadcasted_iota(jnp.int32, (span_size, span_size), 1)
+        allowed = jnp.logical_and(column <= row, column < size)
+        for g in range(GROUPS):
+            query = turn(projected[:, g * HEAD : (g + 1) * HEAD]).astype(jnp.bfloat16)
+            scores = lax.dot_general(
+                query, key, (((1,), (1,)), ((), ())), preferred_element_type=jnp.float32
+            ) * scale
+            scores = jnp.where(allowed, scores, -1e30)
+            raised = jnp.exp(scores - jnp.max(scores, axis=-1, keepdims=True))
+            probs = (raised / jnp.sum(raised, axis=-1, keepdims=True)).astype(jnp.bfloat16)
+            own[here, g * HEAD : (g + 1) * HEAD] = jnp.dot(
+                probs, value, preferred_element_type=jnp.float32
+            ).astype(jnp.bfloat16)
+        send_own(own, gathered, g_send, g_recv, g_own, n)
+
+        @pl.when(n >= 1)
+        def _():
+            relay(gathered, g_send, g_recv, n - 1, pieces)
+
+        @pl.when(n >= 2)
+        def _():
+            relay_far(gathered, g_send, g_recv, n - 2)
+
+        return carry
+
+    half_way = pieces // 2
+    lax.fori_loop(0, half_way, one_span, 0)
+    for c in range(G // 2):
+        forward(wo, zo_send, zo_recv, 1, c)
+    lax.fori_loop(half_way, pieces, one_span, 0)
+    for p in range(inner):
+        for stage, target, ss, rs in (
+            (keys, key_out, k_send, k_recv),
+            (values, value_out, v_send, v_recv),
+        ):
+            near, far = chunk_copy(stage, target, ss, rs, p)
+            pl.when(i == p)(near.start)
+            pl.when(i != p)(far.start)
+    relay(gathered, g_send, g_recv, pieces - 1, pieces)
+    relay_far(gathered, g_send, g_recv, pieces - 2)
+    for s in range(2, line_size - 1):
+        for c in range(G // 2):
+            forward(wo, zo_send, zo_recv, s, c)
+    relay_far(gathered, g_send, g_recv, pieces - 1)
+
+    def fetch(n):
+        return pltpu.make_async_copy(
+            gathered.at[:, pl.ds(pl.multiple_of(n * span_size, span_size), span_size), :],
+            buffer.at[n % 2],
+            load.at[n % 2],
+        )
+
+    def deliver(n):
+        p, part = lax.div(n, spans), n % spans
+        src = mine(result, n)
+        dst = out.at[
+            pl.ds(pl.multiple_of(part * span_size, span_size), span_size),
+            pl.ds(pl.multiple_of(i * QC, HEAD), QC),
+        ]
+        return (
+            p,
+            pltpu.make_async_copy(src, dst, r_send.at[n]),
+            remote(src, dst, r_send.at[n], r_recv.at[i, part], (o * inner + p, t)),
+        )
+
+    settle(own, gathered, g_send, g_recv, g_own, 0)
+    fetch(0).start()
+    for c in range(G // 2):
+        forward(wo, zo_send, zo_recv, line_size - 1, c)
+
+    def one_tile(n, carry):
+        @pl.when(n + 1 < pieces)
+        def _():
+            settle(own, gathered, g_send, g_recv, g_own, n + 1)
+            fetch(n + 1).start()
+
+        fetch(n).wait()
+        total = jnp.zeros((span_size, QC), jnp.float32)
+        for m in range(G):
+            head = (m % slices) * inner + m // slices
+            total = total + jnp.dot(
+                buffer[n % 2, m], wo[pl.ds(head * QC, QC), :], preferred_element_type=jnp.float32
+            )
+        result[pl.ds(pl.multiple_of(n * span_size, span_size), span_size), :] = total.astype(
+            jnp.bfloat16
+        )
+        p, near, far = deliver(n)
+        pl.when(i == p)(near.start)
+        pl.when(i != p)(far.start)
+        return carry
+
+    lax.fori_loop(0, pieces, one_tile, 0)
+
+    hops_sent(wq, zq_send, zq_recv)
+    hops_sent(wo, zo_send, zo_recv)
+    for d in range(1, G):
+        trade(joined, wq, a_send, a_recv, d).wait_send()
+        trade(outs, wo, b_send, b_recv, d).wait_send()
+    for n in range(spans):
+        sent(tokens, t_send, t_recv, n)
+
+    def last(n, carry):
+        sent(gathered, g_send, g_recv, n)
+        p, near, far = deliver(n)
+        pl.when(i == p)(near.wait)
+        pl.when(i != p)(far.wait_send)
+        return carry
+
+    lax.fori_loop(0, pieces, last, 0)
+    for p in range(inner):
+        for stage, target, ss, rs in (
+            (keys, key_out, k_send, k_recv),
+            (values, value_out, v_send, v_recv),
+        ):
+            near, far = chunk_copy(stage, target, ss, rs, p)
+            pl.when(i == p)(near.wait)
+
+            @pl.when(i != p)
+            def _():
+                far.wait_send()
+                chunk_arrived(stage, target, ss, rs, p)
+
+        @pl.when(i != p)
+        def _():
+            for part in range(spans):
+                dst = out.at[pl.ds(part * span_size, span_size), pl.ds(p * QC, QC)]
+                remote(
+                    mine(result, 0), dst, r_send.at[0], r_recv.at[p, part], (o * inner + p, t)
+                ).wait_recv()
+
+
+def fused(members, slices, spans, span_size, normed, joined, outs, bias, cosine, sine, length):
+    inner = G // slices
+    line_size = members // inner
+    token_rows, features = normed.shape
+    rows = joined.shape[1]
+    depth = members * slices * rows
+    every = inner * token_rows
+    pieces = inner * spans
+    bf16 = jnp.bfloat16
+    dma = pltpu.SemaphoreType.DMA
+    hops = [dma((2, line_size, G // 2)), dma((line_size, G // 2))]
+    anywhere = pl.BlockSpec(memory_space=pl.ANY)
+    vmem = pl.BlockSpec(memory_space=pltpu.VMEM)
+    return pl.pallas_call(
+        functools.partial(body, members, slices, spans, span_size),
+        out_shape=[
+            jax.ShapeDtypeStruct((token_rows, inner * QC), bf16),
+            jax.ShapeDtypeStruct((token_rows, inner * HEAD), bf16),
+            jax.ShapeDtypeStruct((token_rows, inner * HEAD), bf16),
+            jax.ShapeDtypeStruct((G, every, QC), bf16),
+        ],
+        in_specs=[anywhere] * 3 + [vmem] * 3 + [pl.BlockSpec(memory_space=pltpu.SMEM)],
+        out_specs=[anywhere] * 4,
+        scratch_shapes=[
+            pltpu.VMEM((depth, QC + 2 * HEAD), bf16),
+            pltpu.VMEM((depth, QC), bf16),
+            pltpu.VMEM((G, token_rows, features), bf16),
+            pltpu.VMEM((every, QC), bf16),
+            pltpu.VMEM((every, HEAD), bf16),
+            pltpu.VMEM((every, HEAD), bf16),
+            pltpu.VMEM((every, QC), bf16),
+            pltpu.VMEM((2, G, span_size, QC), bf16),
+            dma((G,)), dma((G,)), dma,
+            dma((G,)), dma((G,)), dma,
+            *hops, *hops,
+            dma((7, spans)), dma((7, spans)), dma((spans,)),
+            dma((7, pieces)), dma((7, pieces)), dma((pieces,)),
+            dma((2,)),
+            dma((pieces,)), dma((inner, spans)),
+            dma((inner,)), dma((inner,)),
+            dma((inner,)), dma((inner,)),
+        ],
+        compiler_params=pltpu.CompilerParams(
+            collective_id=0, has_side_effects=True, vmem_limit_bytes=61 * 1024 * 1024
+        ),
+    )(normed, joined, outs, bias, cosine, sine, length)
 
 
 def local(
@@ -114,9 +530,7 @@
     joined = jnp.concatenate(
         [blocks(query_weight), blocks(key_weight), blocks(value_weight)], axis=2
     )
-    weight = gather_line(exchange(joined))
-    out_whole = gather_line(exchange(blocks(out_weight)))
-
+    out_blocks = blocks(out_weight)
     source = hidden_in.astype(jnp.float32)
     squares = jnp.sum(source * source, axis=-1, keepdims=True)
     bit = 1
@@ -126,9 +540,6 @@
     inverse_rms = lax.rsqrt(squares / (features * slices) + epsilon)
     gain = lax.dynamic_slice_in_dim(norm_gain, t * features, features).astype(jnp.float32)
     normed = (source * inverse_rms * gain).astype(jnp.bfloat16)
-    tokens = gather_group(normed)
-    spans = lax.all_gather(jnp.stack([span_start, span_length]), "fsdp", axis=1, tiled=True)
-
     bias = jnp.concatenate(
         [
             lax.dynamic_slice_in_dim(query_bias, i * qc, qc),
@@ -136,6 +547,25 @@
             lax.dynamic_slice_in_dim(value_bias, i * HEAD, HEAD),
         ]
     ).astype(jnp.float32)
+    marks = jnp.stack([span_start, span_length])
+    marks = [marks] + [xor(marks, ki * slices) for ki in range(1, inner)]
+    if learner_rows % 16 == 0 and outer >= 3:
+        marks = jnp.concatenate(unswap(marks), axis=1)
+        cosine, sine = angles(marks[0], span_size)
+        cosine, sine = cosine[:, 0], sine[:, 0]
+        return tuple(
+            fused(
+                members, slices, local_spans, span_size, normed, joined, out_blocks,
+                bias[None, :],
+                jnp.concatenate([cosine, cosine], axis=1),
+                jnp.concatenate([-sine, sine], axis=1),
+                marks[1],
+            )[:3]
+        )
+
+    tokens = gather_group(normed)
+    weight = gather_line(exchange(joined))
+    out_whole = gather_line(exchange(out_blocks))
     rows = jnp.arange(span_size, dtype=jnp.int32)[:, None]
     columns = jnp.arange(span_size, dtype=jnp.int32)[None, :]
     halves = [
@@ -148,10 +578,7 @@
             projected = projected + jnp.dot(
                 tokens[ki * slices + kt], halves[kt], preferred_element_type=jnp.float32
             )
-        own = lax.dynamic_slice_in_dim(
-            spans, (line * inner + (i ^ ki)) * local_spans, local_spans, axis=1
-        )
-        start, length = own[0], own[1]
+        start, length = marks[ki][0], marks[ki][1]
         cosine, sine = angles(start, span_size)
         query = rotate(
             projected[:, :qc].reshape(token_rows, GROUPS, HEAD), cosine, sine

time: 645 us -> 378 us (0.59); the launches traced: 636 us -> 378 us
  Pallas kernels: 0 us -> 343 us
  waiting for transfers between devices: 228 us -> 0.01 us
  matrix products: 121 us -> 0 us
  local copies, waits for them, and re-layouts: 112 us -> 14.8 us
  blocking collectives: 85.9 us -> 0 us
  starting transfers between devices: 58.9 us -> 4.97 us
  other arithmetic: 27.9 us -> 14.5 us
    pallas_call x0 -> x1, Pallas kernels: none -> 343 us  [fused(): pl.pallas_call(functools.partial(body, members, slices, spans, span_size)...]
    ppermute x12 -> x0, waiting for transfers between devices: 116 us -> none  [shift(): return lax.ppermute(x, AXES, pairs)]
    ppermute x26 -> x4, waiting for transfers between devices: 112 us -> 0.01 us  [xor(): return lax.ppermute(x, AXES, [(d, d ^ k) for d in range(devices)])]
    dot_general x20 -> x0, matrix products: 104 us -> none  [the longest x8 56.5 us: local(): jnp.dot(attended[k], lax.dynamic_slice_in_dim(out_whole, head * qc, qc),...]
    all_gather x1 -> x0, blocking collectives: 52.8 us -> none  [local(): lax.all_gather(jnp.stack([span_start, span_length]), 'fsdp', axis=1, tile...]
    ppermute x12 -> x0, starting transfers between devices: 37.1 us -> none  [shift(): return lax.ppermute(x, AXES, pairs)]
    unnamed x102 -> x26, local copies, waits for them, and re-layouts: 41.3 us -> 5.26 us
    all_to_all x1 -> x0, blocking collectives: 33.1 us -> none  [exchange(): lax.all_to_all(stacked, AXES, split_axis=0, concat_axis=0, axis_index_gro...]
  transfers between devices with their start and end apart: 39 -> 4, of which waited for: 13 -> 0; matrix products, arithmetic and copies ran while one was open for 37% -> 6% of each run, Pallas kernels for 0% -> 0%
where the time goes in v2:
time: 378 us
  Pallas kernels  343 us (91%)
  local copies, waits for them, and re-layouts  14.8 us (4%)
  other arithmetic  14.5 us (4%)
  starting transfers between devices  4.97 us (1%)
    pallas_call x1, Pallas kernels, fused(): pl.pallas_call(functools.partial(body, members, slices, spans, span_size)...  343 us
    reshape x8, local copies, waits for them, and re-layouts, blocks(): cut = weight.reshape(learner_rows, slices, inner, cols)  8.16 us
  transfers between devices with their start and end apart: 4, of which 0 were waited for; matrix products, arithmetic and copies ran while one was open for 6% of the time, Pallas kernels for 0%

profile of v2, /device:TPU:0, one launch (start us, length us, event | category | flops | bytes accessed | tf_op | source)
XLA Modules:
  0.0 378.0 jit_solution(12352979178305338657)
XLA Ops:
  0.7 0.7 pad_add_fusion
  1.4 0.5 collective-permute-start.3
  1.9 2.6 collective-permute-start.2
  4.6 2.3 fusion
  6.9 1.8 collective-permute-start
  8.7 0.8 dynamic_slice.13
  9.5 0.2 reshape.97
  9.7 0.8 copy.19
  10.5 0.2 reshape.99
  10.7 0.8 copy.20
  11.5 1.3 reshape.95
  12.7 0.2 copy.18
  13.0 3.3 reshape.101
  16.3 1.4 copy.21
  17.9 0.6 maximum_convert_fusion.bias
  18.5 2.7 pad_maximum_fusion.joined
  21.4 0.5 slice_bitcast_fusion
  22.0 3.7 fusion.3
  25.7 2.0 pad_maximum_fusion.1
  27.8 2.2 fusion.2.normed
  30.0 343.0 %shard_map.130 = (bf16[512,2560]{1,0:T(8,128)(2,1)}, bf16[512,512]{1,0:T(8,128)(2,1)}, bf16[512,512]{1,0:T(8,128)(2,1)}, bf16[8,2048,640]{2,1,0:T(8,128)(2,1)}) custom-call(bf16[512,2560]{1,0:T(8,128)(2,1)} %fusion.2.normed, bf16[8,160,896]{2,1,0:T(8,128)(2,1)} %pad_maximum_fusion.joined, bf16[8,160,640]{2,1,0:T(8,128)(2,1)} %bitcast.28, ...), custom_call_target="tpu_custom_call" | custom-call | tf_op jit(solution)/shard_map/pallas_call | solution.py:413
  373.0 3.5 copy.26
  376.5 0.8 copy.27
  377.3 0.8 copy.28
  (36 shorter events, 0.6 us)
Async XLA Ops:
  0.6 8.8 %copy-start.4 = (bf16[160,1024]{1,0:T(8,128)(2,1)S(1)}, bf16[160,1024]{1,0:T(8,128)(2,1)}, u32[]{:S(2)}) copy-start(bf16[160,1024]{1,0:T(8,128)(2,1)} %param.14) | copy-start | bytes 983044
  0.6 9.8 %copy-start.5 = (bf16[160,1024]{1,0:T(8,128)(2,1)S(1)}, bf16[160,1024]{1,0:T(8,128)(2,1)}, u32[]{:S(2)}) copy-start(bf16[160,1024]{1,0:T(8,128)(2,1)} %param.15) | copy-start | bytes 983044
  1.4 10.1 %copy-start.1 = (bf16[160,5120]{1,0:T(8,128)(2,1)S(1)}, bf16[160,5120]{1,0:T(8,128)(2,1)}, u32[]{:S(2)}) copy-start(bf16[160,5120]{1,0:T(8,128)(2,1)} %param.13) | copy-start | bytes 4915204
  1.4 19.8 %collective-permute-start.3 = (s32[2,2]{1,0:T(2,128)S(1)}, s32[2,2]{1,0:T(2,128)S(1)}, u32[]{:S(2)}, u32[]{:S(2)}) collective-permute-start(s32[2,2]{1,0:T(2,128)S(1)} %pad_add_fusion), channel_id=1, source_target_pairs={{0,2},{1,3},{2,0},{3,1},{4,6},{5,7},{6,4},{7,5},{8,10},{9,11},{10,... | collective-permute-start | bytes 56 | tf_op jit(solution)/shard_map/ppermute | solution.py:477
  1.9 19.3 %collective-permute-start.2 = (s32[2,2]{1,0:T(2,128)S(1)}, s32[2,2]{1,0:T(2,128)S(1)}, u32[]{:S(2)}, u32[]{:S(2)}) collective-permute-start(s32[2,2]{1,0:T(2,128)S(1)} %pad_add_fusion), channel_id=1, source_target_pairs={{0,4},{1,5},{2,6},{3,7},{4,0},{5,1},{6,2},{7,3},{8,12},{9,13},{10,... | collective-permute-start | bytes 56 | tf_op jit(solution)/shard_map/ppermute | solution.py:477
  4.5 16.7 %collective-permute-start.1 = (s32[2,2]{1,0:T(2,128)S(1)}, s32[2,2]{1,0:T(2,128)S(1)}, u32[]{:S(2)}, u32[]{:S(2)}) collective-permute-start(s32[2,2]{1,0:T(2,128)S(1)} %pad_add_fusion), channel_id=1, source_target_pairs={{0,6},{1,7},{2,4},{3,5},{4,2},{5,3},{6,0},{7,1},{8,14},{9,15},{10,... | collective-permute-start | bytes 56 | tf_op jit(solution)/shard_map/ppermute | solution.py:477
  6.9 20.8 %collective-permute-start = (f32[512,1]{0,1:T(1,128)S(1)}, f32[512,1]{0,1:T(1,128)S(1)}, u32[]{:S(2)}, u32[]{:S(2)}) collective-permute-start(f32[512,1]{0,1:T(1,128)S(1)} %bitcast.33), channel_id=1, source_target_pairs={{0,1},{1,0},{2,3},{3,2},{4,5},{5,4},{6,7},{7,6},{8,9},{9,8},{10,11... | collective-permute-start | bytes 6152 | tf_op jit(solution)/shard_map/ppermute | solution.py:477
  12.9 4.8 %copy-start.6 = (bf16[5120]{0:T(1024)(128)(2,1)S(1)}, bf16[5120]{0:T(1024)(128)(2,1)}, u32[]{:S(2)}) copy-start(bf16[5120]{0:T(1024)(128)(2,1)} %param.12) | copy-start | bytes 30724
  13.0 4.9 %copy-start.9 = (bf16[512]{0:T(512)(128)(2,1)S(1)}, bf16[512]{0:T(512)(128)(2,1)}, u32[]{:S(2)}) copy-start(bf16[512]{0:T(512)(128)(2,1)} %param.19) | copy-start | bytes 3076
  13.0 4.8 %copy-start.10 = (bf16[512]{0:T(512)(128)(2,1)S(1)}, bf16[512]{0:T(512)(128)(2,1)}, u32[]{:S(2)}) copy-start(bf16[512]{0:T(512)(128)(2,1)} %param.18) | copy-start | bytes 3076
  17.7 3.5 copy-start.7
  17.7 3.5 copy-start.8
  25.7 2.1 copy-start
  372.9 3.5 copy-start.3
  373.0 4.3 %copy-start.2 = (bf16[512,512]{1,0:T(8,128)(2,1)S(1)}, bf16[512,512]{1,0:T(8,128)(2,1)}, u32[]{:S(2)}) copy-start(bf16[512,512]{1,0:T(8,128)(2,1)} %get-tuple-element.27) | copy-start | bytes 1572868

commit v3 on v2

--- a/solution.py
+++ b/solution.py
@@ -44,7 +44,7 @@
 
 def body(
     members, slices, spans, span_size,
-    normed, joined, outs, bias, cosine, sine, length,
+    normed, query_in, key_in, value_in, out_in, bias, cosine, sine, length,
     out, key_out, value_out, gathered,
     wq, wo, tokens, own, keys, values, result, buffer,
     a_send, a_recv, a_own, b_send, b_recv, b_own,
@@ -59,7 +59,7 @@
     o = lax.div(f, inner)
     i = f % inner
     me = i * slices + t
-    rows = joined.shape[1]
+    rows = query_in.shape[0]
     mx, my, mc = flip(me, 4), flip(me, 1), flip(me, 2)
     md = flip(mx, 1)
 
@@ -91,28 +91,47 @@
     def place(buf, origin, m, count):
         return buf.at[pl.ds(pl.multiple_of((origin * G + m) * rows, rows), count * rows), :]
 
-    def trade(src, buf, ss, rs, d):
+    def cut(src, m):
+        cols = src.shape[1] // G
+        head = (m % slices) * inner + lax.div(m, slices)
+        return src.at[:, pl.ds(pl.multiple_of(head * cols, HEAD), cols)]
+
+    def lanes(buf, m, at, cols):
+        return place(buf, o, m, 1).at[:, pl.ds(at, cols)]
+
+    def trade(part, buf, ss, rs, d):
+        k, src, at = part
         to = (me + d) % G
-        return remote(src.at[to], place(buf, o, me, 1), ss.at[d], rs.at[d], member(to))
-
-    def trade_own(src, buf, sem):
-        return pltpu.make_async_copy(src.at[me], place(buf, o, me, 1), sem)
-
-    def trade_start(src, buf, ss, rs, sem):
-        trade_own(src, buf, sem).start()
+        dst = lanes(buf, me, at, src.shape[1] // G)
+        return remote(cut(src, to), dst, ss.at[k, d], rs.at[k, d], member(to))
+
+    def trade_own(part, buf, sem):
+        k, src, at = part
+        dst = lanes(buf, me, at, src.shape[1] // G)
+        return pltpu.make_async_copy(cut(src, me), dst, sem.at[k])
+
+    def trade_start(parts, buf, ss, rs, sem):
         for d in range(1, G):
-            trade(src, buf, ss, rs, d).start()
-
-    def trade_wait(src, buf, ss, rs, sem, m):
+            for part in parts:
+                trade(part, buf, ss, rs, d).start()
+        for part in parts:
+            trade_own(part, buf, sem).start()
+
+    def trade_wait(parts, buf, ss, rs, sem, m):
         @pl.when(m == me)
         def _():
-            trade_own(src, buf, sem).wait()
+            for part in parts:
+                trade_own(part, buf, sem).wait()
 
         @pl.when(m != me)
         def _():
             d = (me - m + G) % G
-            here = place(buf, o, m, 1)
-            remote(here, here, ss.at[d], rs.at[d], member(m)).wait_recv()
+            for k, src, at in parts:
+                here = lanes(buf, m, at, src.shape[1] // G)
+                remote(here, here, ss.at[k, d], rs.at[k, d], member(m)).wait_recv()
+
+    inputs = ((0, query_in, 0), (1, key_in, QC), (2, value_in, QC + HEAD))
+    outs = ((0, out_in, 0),)
 
     def hop(buf, ss, rs, origin, c, way):
         here = place(buf, origin, 2 * c, 2)
@@ -121,7 +140,7 @@
 
     def forward(buf, ss, rs, s, c):
         below, above = o - s, o + s
-        if s > 0:
+        if not isinstance(s, int) or s > 0:
             @pl.when(below >= 0)
             def _():
                 hop(buf, ss, rs, below, c, 0).wait_recv()
@@ -138,18 +157,19 @@
         def _():
             hop(buf, ss, rs, above, c, 1).start()
 
-    def hops_sent(buf, ss, rs):
-        for s in range(line_size):
-            for c in range(G // 2):
-                below, above = o - s, o + s
-
-                @pl.when(jnp.logical_and(below >= 0, o < line_size - 1))
-                def _():
-                    hop(buf, ss, rs, below, c, 0).wait_send()
-
-                @pl.when(jnp.logical_and(above < line_size, o > 0))
-                def _():
-                    hop(buf, ss, rs, above, c, 1).wait_send()
+    def hops_sent(buf, ss, rs, s):
+        below, above = o - s, o + s
+        for c in range(G // 2):
+            hop_sent(buf, ss, rs, below, above, c)
+
+    def hop_sent(buf, ss, rs, below, above, c):
+        @pl.when(jnp.logical_and(below >= 0, o < line_size - 1))
+        def _():
+            hop(buf, ss, rs, below, c, 0).wait_send()
+
+        @pl.when(jnp.logical_and(above < line_size, o > 0))
+        def _():
+            hop(buf, ss, rs, above, c, 1).wait_send()
 
     def piece(buf, m, n):
         return buf.at[m, pl.ds(pl.multiple_of(n * span_size, span_size), span_size), :]
@@ -201,30 +221,32 @@
             here = piece(buf, me, n)
             remote(here, here, ss.at[kind, n], rs.at[kind, n], member(mx)).wait_send()
 
-    trade_start(joined, wq, a_send, a_recv, a_own)
+    trade_start(inputs, wq, a_send, a_recv, a_own)
     for n in range(spans):
         send_own(normed, tokens, t_send, t_recv, t_own, n)
     for c in range(G // 2):
         for m in (2 * c, 2 * c + 1):
-            trade_wait(joined, wq, a_send, a_recv, a_own, m)
+            trade_wait(inputs, wq, a_send, a_recv, a_own, m)
         forward(wq, zq_send, zq_recv, 0, c)
+    for c in range(G // 2):
+        forward(wq, zq_send, zq_recv, 1, c)
     for n in range(spans):
         relay(tokens, t_send, t_recv, n, spans)
-    for c in range(G // 2):
-        forward(wq, zq_send, zq_recv, 1, c)
     trade_start(outs, wo, b_send, b_recv, b_own)
-    for n in range(spans):
-        relay_far(tokens, t_send, t_recv, n)
-    for s in range(2, line_size):
-        if s == line_size - 1:
-            for c in range(G // 2):
-                for m in (2 * c, 2 * c + 1):
-                    trade_wait(outs, wo, b_send, b_recv, b_own, m)
-                forward(wo, zo_send, zo_recv, 0, c)
+    for s in range(2, line_size - 1):
         for c in range(G // 2):
             forward(wq, zq_send, zq_recv, s, c)
     for n in range(spans):
+        relay_far(tokens, t_send, t_recv, n)
+    for m in range(G):
+        trade_wait(outs, wo, b_send, b_recv, b_own, m)
+    for c in range(G // 2):
+        hop_sent(wq, zq_send, zq_recv, o - (line_size - 2), o + (line_size - 2), c)
+        forward(wo, zo_send, zo_recv, 0, c)
+    for n in range(spans):
         settle(normed, tokens, t_send, t_recv, t_own, n)
+    for c in range(G // 2):
+        forward(wq, zq_send, zq_recv, line_size - 1, c)
 
     pieces = inner * spans
     features = tokens.shape[2]
@@ -280,6 +302,7 @@
                 probs, value, preferred_element_type=jnp.float32
             ).astype(jnp.bfloat16)
         send_own(own, gathered, g_send, g_recv, g_own, n)
+        forward(wo, zo_send, zo_recv, 1 + lax.div(n, G // 2), n % (G // 2))
 
         @pl.when(n >= 1)
         def _():
@@ -291,11 +314,7 @@
 
         return carry
 
-    half_way = pieces // 2
-    lax.fori_loop(0, half_way, one_span, 0)
-    for c in range(G // 2):
-        forward(wo, zo_send, zo_recv, 1, c)
-    lax.fori_loop(half_way, pieces, one_span, 0)
+    lax.fori_loop(0, pieces, one_span, 0)
     for p in range(inner):
         for stage, target, ss, rs in (
             (keys, key_out, k_send, k_recv),
@@ -306,9 +325,6 @@
             pl.when(i != p)(far.start)
     relay(gathered, g_send, g_recv, pieces - 1, pieces)
     relay_far(gathered, g_send, g_recv, pieces - 2)
-    for s in range(2, line_size - 1):
-        for c in range(G // 2):
-            forward(wo, zo_send, zo_recv, s, c)
     relay_far(gathered, g_send, g_recv, pieces - 1)
 
     def fetch(n):
@@ -333,8 +349,9 @@
 
     settle(own, gathered, g_send, g_recv, g_own, 0)
     fetch(0).start()
-    for c in range(G // 2):
-        forward(wo, zo_send, zo_recv, line_size - 1, c)
+    for s in range(1 + pieces // (G // 2), line_size):
+        for c in range(G // 2):
+            forward(wo, zo_send, zo_recv, s, c)
 
     def one_tile(n, carry):
         @pl.when(n + 1 < pieces)
@@ -359,11 +376,15 @@
 
     lax.fori_loop(0, pieces, one_tile, 0)
 
-    hops_sent(wq, zq_send, zq_recv)
-    hops_sent(wo, zo_send, zo_recv)
+    for s in range(line_size):
+        if s != line_size - 2:
+            hops_sent(wq, zq_send, zq_recv, s)
+        hops_sent(wo, zo_send, zo_recv, s)
     for d in range(1, G):
-        trade(joined, wq, a_send, a_recv, d).wait_send()
-        trade(outs, wo, b_send, b_recv, d).wait_send()
+        for part in inputs:
+            trade(part, wq, a_send, a_recv, d).wait_send()
+        for part in outs:
+            trade(part, wo, b_send, b_recv, d).wait_send()
     for n in range(spans):
         sent(tokens, t_send, t_recv, n)
 
@@ -397,11 +418,11 @@
                 ).wait_recv()
 
 
-def fused(members, slices, spans, span_size, normed, joined, outs, bias, cosine, sine, length):
+def fused(members, slices, spans, span_size, normed, weights, bias, cosine, sine, length):
     inner = G // slices
     line_size = members // inner
     token_rows, features = normed.shape
-    rows = joined.shape[1]
+    rows = weights[0].shape[0]
     depth = members * slices * rows
     every = inner * token_rows
     pieces = inner * spans
@@ -418,7 +439,7 @@
             jax.ShapeDtypeStruct((token_rows, inner * HEAD), bf16),
             jax.ShapeDtypeStruct((G, every, QC), bf16),
         ],
-        in_specs=[anywhere] * 3 + [vmem] * 3 + [pl.BlockSpec(memory_space=pltpu.SMEM)],
+        in_specs=[anywhere] * 5 + [vmem] * 3 + [pl.BlockSpec(memory_space=pltpu.SMEM)],
         out_specs=[anywhere] * 4,
         scratch_shapes=[
             pltpu.VMEM((depth, QC + 2 * HEAD), bf16),
@@ -429,8 +450,8 @@
             pltpu.VMEM((every, HEAD), bf16),
             pltpu.VMEM((every, QC), bf16),
             pltpu.VMEM((2, G, span_size, QC), bf16),
-            dma((G,)), dma((G,)), dma,
-            dma((G,)), dma((G,)), dma,
+            dma((3, G)), dma((3, G)), dma((3,)),
+            dma((1, G)), dma((1, G)), dma((1,)),
             *hops, *hops,
             dma((7, spans)), dma((7, spans)), dma((spans,)),
             dma((7, pieces)), dma((7, pieces)), dma((pieces,)),
@@ -442,7 +463,7 @@
         compiler_params=pltpu.CompilerParams(
             collective_id=0, has_side_effects=True, vmem_limit_bytes=61 * 1024 * 1024
         ),
-    )(normed, joined, outs, bias, cosine, sine, length)
+    )(normed, *weights, bias, cosine, sine, length)
 
 
 def local(
@@ -555,7 +576,8 @@
         cosine, sine = cosine[:, 0], sine[:, 0]
         return tuple(
             fused(
-                members, slices, local_spans, span_size, normed, joined, out_blocks,
+                members, slices, local_spans, span_size, normed,
+                (query_weight, key_weight, value_weight, out_weight),
                 bias[None, :],
                 jnp.concatenate([cosine, cosine], axis=1),
                 jnp.concatenate([-sine, sine], axis=1),

time: 378 us -> 363 us (0.960); the launches traced: 378 us -> 357 us
  Pallas kernels: 343 us -> 333 us
  local copies, waits for them, and re-layouts: 14.8 us -> 6.56 us
    pallas_call x1, Pallas kernels: 343 us -> 333 us  [fused(): pl.pallas_call(functools.partial(body, members, slices, spans, span_size)...]
    reshape x8 -> x0, local copies, waits for them, and re-layouts: 8.16 us -> none  [blocks(): cut = weight.reshape(learner_rows, slices, inner, cols)]
  transfers between devices with their start and end apart: 4 -> 4, of which waited for: 0 -> 0; matrix products, arithmetic and copies ran while one was open for 6% -> 3% of each run, Pallas kernels for 0% -> 0%
where the time goes in v3:
time: 363 us; the launch traced here: 357 us
  Pallas kernels  333 us (92%)
  other arithmetic  11.8 us (3%)
  local copies, waits for them, and re-layouts  6.56 us (2%)
  starting transfers between devices  4.89 us (1%)
    pallas_call x1, Pallas kernels, fused(): pl.pallas_call(functools.partial(body, members, slices, spans, span_size)...  333 us
  transfers between devices with their start and end apart: 4, of which 0 were waited for; matrix products, arithmetic and copies ran while one was open for 3% of the time, Pallas kernels for 0%

profile of v3, /device:TPU:0, one launch (start us, length us, event | category | flops | bytes accessed | tf_op | source)
XLA Modules:
  0.0 357.1 jit_solution(13145490490725908764)
XLA Ops:
  0.7 0.7 pad_add_fusion
  1.4 0.5 collective-permute-start.3
  1.8 2.6 collective-permute-start.2
  4.4 0.1 collective-permute-start.1
  4.5 2.3 fusion
  6.8 1.8 collective-permute-start
  8.6 0.8 dynamic_slice.13
  9.4 0.1 dynamic-slice_convert_fusion
  9.5 0.1 dynamic-slice_bitcast_fusion
  9.6 0.6 maximum_convert_fusion.bias
  10.1 0.0 collective-permute-done.3
  10.1 0.0 collective-permute-done.2
  10.2 0.1 pad_add_fusion.1
  10.3 0.5 slice_bitcast_fusion
  10.8 0.1 convert_bitcast_fusion
  10.9 3.7 %fusion.3 = (f32[2048,64]{1,0:T(8,128)S(1)}, f32[2048,64]{1,0:T(8,128)S(1)}, f32[2048,64]{1,0:T(8,128)S(1)}) fusion(f32[64]{0:T(128)S(1)} %negate_power_fusion, f32[2048]{0:T(1024)S(1)} %bitcast.15), kind=kLoop, calls=%fused_computation.9 | loop fusion | flops 262144 | bytes 1581312 | tf_op jit(solution)/shard_map/neg | solution.py:583
  14.6 0.0 copy-start
  14.6 2.0 pad_maximum_fusion
  16.6 0.1 copy-done
  16.7 2.2 fusion.2.normed
  18.9 333.1 %shard_map.130 = (bf16[512,2560]{1,0:T(8,128)(2,1)}, bf16[512,512]{1,0:T(8,128)(2,1)}, bf16[512,512]{1,0:T(8,128)(2,1)}, bf16[8,2048,640]{2,1,0:T(8,128)(2,1)}) custom-call(bf16[512,2560]{1,0:T(8,128)(2,1)} %fusion.2.normed, bf16[160,5120]{1,0:T(8,128)(2,1)} %query_in.1, bf16[160,1024]{1,0:T(8,128)(2,1)} %key_in.1, bf16[160,1024]{1,0:T(8,128)(2,1)} %value_in.1, ...), custom_call_target="tpu_custom_call" | custom-call | tf_op jit(solution)/shard_map/pallas_call | solution.py:434
  352.0 3.5 copy.18
  355.5 0.8 copy.19
  356.3 0.8 copy.20
  (21 shorter events, 0.1 us)
Async XLA Ops:
  0.6 9.5 %copy-start.4 = (s32[2]{0:T(128)S(1)}, s32[2]{0:T(128)}, u32[]{:S(2)}) copy-start(s32[2]{0:T(128)} %param.21) | copy-start | bytes 28
  0.6 9.5 %copy-start.5 = (s32[2]{0:T(128)S(1)}, s32[2]{0:T(128)}, u32[]{:S(2)}) copy-start(s32[2]{0:T(128)} %param.20) | copy-start | bytes 28
  0.7 8.7 %copy-start.3 = (bf16[5120]{0:T(1024)(128)(2,1)S(1)}, bf16[5120]{0:T(1024)(128)(2,1)}, u32[]{:S(2)}) copy-start(bf16[5120]{0:T(1024)(128)(2,1)} %param.12) | copy-start | bytes 30724
  0.7 8.8 %copy-start.6 = (bf16[512]{0:T(512)(128)(2,1)S(1)}, bf16[512]{0:T(512)(128)(2,1)}, u32[]{:S(2)}) copy-start(bf16[512]{0:T(512)(128)(2,1)} %param.19) | copy-start | bytes 3076
  0.7 8.8 %copy-start.7 = (bf16[512]{0:T(512)(128)(2,1)S(1)}, bf16[512]{0:T(512)(128)(2,1)}, u32[]{:S(2)}) copy-start(bf16[512]{0:T(512)(128)(2,1)} %param.18) | copy-start | bytes 3076
  1.4 8.8 %collective-permute-start.3 = (s32[2,2]{1,0:T(2,128)S(1)}, s32[2,2]{1,0:T(2,128)S(1)}, u32[]{:S(2)}, u32[]{:S(2)}) collective-permute-start(s32[2,2]{1,0:T(2,128)S(1)} %pad_add_fusion), channel_id=1, source_target_pairs={{0,2},{1,3},{2,0},{3,1},{4,6},{5,7},{6,4},{7,5},{8,10},{9,11},{10,... | collective-permute-start | bytes 56 | tf_op jit(solution)/shard_map/ppermute | solution.py:498
  1.8 8.3 %collective-permute-start.2 = (s32[2,2]{1,0:T(2,128)S(1)}, s32[2,2]{1,0:T(2,128)S(1)}, u32[]{:S(2)}, u32[]{:S(2)}) collective-permute-start(s32[2,2]{1,0:T(2,128)S(1)} %pad_add_fusion), channel_id=1, source_target_pairs={{0,4},{1,5},{2,6},{3,7},{4,0},{5,1},{6,2},{7,3},{8,12},{9,13},{10,... | collective-permute-start | bytes 56 | tf_op jit(solution)/shard_map/ppermute | solution.py:498
  4.4 5.8 %collective-permute-start.1 = (s32[2,2]{1,0:T(2,128)S(1)}, s32[2,2]{1,0:T(2,128)S(1)}, u32[]{:S(2)}, u32[]{:S(2)}) collective-permute-start(s32[2,2]{1,0:T(2,128)S(1)} %pad_add_fusion), channel_id=1, source_target_pairs={{0,6},{1,7},{2,4},{3,5},{4,2},{5,3},{6,0},{7,1},{8,14},{9,15},{10,... | collective-permute-start | bytes 56 | tf_op jit(solution)/shard_map/ppermute | solution.py:498
  6.8 9.8 %collective-permute-start = (f32[512,1]{0,1:T(1,128)S(1)}, f32[512,1]{0,1:T(1,128)S(1)}, u32[]{:S(2)}, u32[]{:S(2)}) collective-permute-start(f32[512,1]{0,1:T(1,128)S(1)} %bitcast.17), channel_id=1, source_target_pairs={{0,1},{1,0},{2,3},{3,2},{4,5},{5,4},{6,7},{7,6},{8,9},{9,8},{10,11... | collective-permute-start | bytes 6152 | tf_op jit(solution)/shard_map/ppermute | solution.py:498
  14.6 2.1 copy-start
  352.0 3.5 copy-start.2
  352.0 4.3 %copy-start.1 = (bf16[512,512]{1,0:T(8,128)(2,1)S(1)}, bf16[512,512]{1,0:T(8,128)(2,1)}, u32[]{:S(2)}) copy-start(bf16[512,512]{1,0:T(8,128)(2,1)} %get-tuple-element.27) | copy-start | bytes 1572868

commit v4 on v3

--- a/solution.py
+++ b/solution.py
@@ -46,7 +46,7 @@
     members, slices, spans, span_size,
     normed, query_in, key_in, value_in, out_in, bias, cosine, sine, length,
     out, key_out, value_out, gathered,
-    wq, wo, tokens, own, keys, values, result, buffer,
+    wq, wo, tokens, own, keys, values, result, buffer, partial,
     a_send, a_recv, a_own, b_send, b_recv, b_own,
     zq_send, zq_recv, zo_send, zo_recv,
     t_send, t_recv, t_own, g_send, g_recv, g_own,
@@ -111,22 +111,18 @@
         return pltpu.make_async_copy(cut(src, me), dst, sem.at[k])
 
     def trade_start(parts, buf, ss, rs, sem):
+        for part in parts:
+            trade_own(part, buf, sem).start()
         for d in range(1, G):
             for part in parts:
                 trade(part, buf, ss, rs, d).start()
-        for part in parts:
-            trade_own(part, buf, sem).start()
-
-    def trade_wait(parts, buf, ss, rs, sem, m):
-        @pl.when(m == me)
-        def _():
-            for part in parts:
-                trade_own(part, buf, sem).wait()
-
-        @pl.when(m != me)
-        def _():
-            d = (me - m + G) % G
-            for k, src, at in parts:
+
+    def trade_wait(parts, buf, ss, rs, sem, d):
+        m = (me + G - d) % G
+        for k, src, at in parts:
+            if d == 0:
+                trade_own((k, src, at), buf, sem).wait()
+            else:
                 here = lanes(buf, m, at, src.shape[1] // G)
                 remote(here, here, ss.at[k, d], rs.at[k, d], member(m)).wait_recv()
 
@@ -134,7 +130,7 @@
     outs = ((0, out_in, 0),)
 
     def hop(buf, ss, rs, origin, c, way):
-        here = place(buf, origin, 2 * c, 2)
+        here = place(buf, origin, (me + G - c) % G, 1)
         way_f = f + inner if way == 0 else f - inner
         return remote(here, here, ss.at[way, origin, c], rs.at[origin, c], (way_f, t))
 
@@ -159,7 +155,7 @@
 
     def hops_sent(buf, ss, rs, s):
         below, above = o - s, o + s
-        for c in range(G // 2):
+        for c in range(G):
             hop_sent(buf, ss, rs, below, above, c)
 
     def hop_sent(buf, ss, rs, below, above, c):
@@ -222,30 +218,30 @@
             remote(here, here, ss.at[kind, n], rs.at[kind, n], member(mx)).wait_send()
 
     trade_start(inputs, wq, a_send, a_recv, a_own)
-    for n in range(spans):
-        send_own(normed, tokens, t_send, t_recv, t_own, n)
-    for c in range(G // 2):
-        for m in (2 * c, 2 * c + 1):
-            trade_wait(inputs, wq, a_send, a_recv, a_own, m)
+    for c in range(G):
+        trade_wait(inputs, wq, a_send, a_recv, a_own, c)
         forward(wq, zq_send, zq_recv, 0, c)
-    for c in range(G // 2):
+        if c == 0:
+            for n in range(spans):
+                send_own(normed, tokens, t_send, t_recv, t_own, n)
+    for c in range(G):
         forward(wq, zq_send, zq_recv, 1, c)
     for n in range(spans):
         relay(tokens, t_send, t_recv, n, spans)
     trade_start(outs, wo, b_send, b_recv, b_own)
     for s in range(2, line_size - 1):
-        for c in range(G // 2):
+        for c in range(G):
             forward(wq, zq_send, zq_recv, s, c)
     for n in range(spans):
         relay_far(tokens, t_send, t_recv, n)
     for m in range(G):
         trade_wait(outs, wo, b_send, b_recv, b_own, m)
-    for c in range(G // 2):
+    for c in range(G):
         hop_sent(wq, zq_send, zq_recv, o - (line_size - 2), o + (line_size - 2), c)
         forward(wo, zo_send, zo_recv, 0, c)
     for n in range(spans):
         settle(normed, tokens, t_send, t_recv, t_own, n)
-    for c in range(G // 2):
+    for c in range(G):
         forward(wq, zq_send, zq_recv, line_size - 1, c)
 
     pieces = inner * spans
@@ -302,7 +298,9 @@
                 probs, value, preferred_element_type=jnp.float32
             ).astype(jnp.bfloat16)
         send_own(own, gathered, g_send, g_recv, g_own, n)
-        forward(wo, zo_send, zo_recv, 1 + lax.div(n, G // 2), n % (G // 2))
+        for half in range(2):
+            turn_c = (2 * n + half) % G
+            forward(wo, zo_send, zo_recv, 1 + lax.div(2 * n, G), turn_c)
 
         @pl.when(n >= 1)
         def _():
@@ -349,11 +347,20 @@
 
     settle(own, gathered, g_send, g_recv, g_own, 0)
     fetch(0).start()
-    for s in range(1 + pieces // (G // 2), line_size):
-        for c in range(G // 2):
-            forward(wo, zo_send, zo_recv, s, c)
-
-    def one_tile(n, carry):
+    for n in range(spans):
+        sent(tokens, t_send, t_recv, n)
+
+    far = jnp.where(o < line_size // 2, line_size - 1, 0)
+    per = G // line_size
+
+    def head_of(slab, e):
+        head = slab * per + e
+        return (
+            (head % inner) * slices + lax.div(head, inner),
+            wo[pl.ds(pl.multiple_of(head * QC, QC), QC), :],
+        )
+
+    def near_tile(n, carry):
         @pl.when(n + 1 < pieces)
         def _():
             settle(own, gathered, g_send, g_recv, g_own, n + 1)
@@ -361,20 +368,41 @@
 
         fetch(n).wait()
         total = jnp.zeros((span_size, QC), jnp.float32)
-        for m in range(G):
-            head = (m % slices) * inner + m // slices
+        for j in range(1, line_size):
+            for e in range(per):
+                m, weight = head_of((far + j) % line_size, e)
+                total = total + jnp.dot(
+                    buffer[n % 2, m], weight, preferred_element_type=jnp.float32
+                )
+        partial[n] = total
+        for e in range(per):
+            m, _ = head_of(far, e)
+            tokens[n, e * span_size : (e + 1) * span_size, :QC] = buffer[n % 2, m]
+        return carry
+
+    lax.fori_loop(0, pieces, near_tile, 0)
+    for s in range(1 + 2 * pieces // G, line_size):
+        for c in range(G):
+            forward(wo, zo_send, zo_recv, s, c)
+
+    def far_tile(n, carry):
+        total = partial[n]
+        for e in range(per):
+            _, weight = head_of(far, e)
             total = total + jnp.dot(
-                buffer[n % 2, m], wo[pl.ds(head * QC, QC), :], preferred_element_type=jnp.float32
+                tokens[n, e * span_size : (e + 1) * span_size, :QC],
+                weight,
+                preferred_element_type=jnp.float32,
             )
         result[pl.ds(pl.multiple_of(n * span_size, span_size), span_size), :] = total.astype(
             jnp.bfloat16
         )
-        p, near, far = deliver(n)
+        p, near, away = deliver(n)
         pl.when(i == p)(near.start)
-        pl.when(i != p)(far.start)
+        pl.when(i != p)(away.start)
         return carry
 
-    lax.fori_loop(0, pieces, one_tile, 0)
+    lax.fori_loop(0, pieces, far_tile, 0)
 
     for s in range(line_size):
         if s != line_size - 2:
@@ -385,8 +413,6 @@
             trade(part, wq, a_send, a_recv, d).wait_send()
         for part in outs:
             trade(part, wo, b_send, b_recv, d).wait_send()
-    for n in range(spans):
-        sent(tokens, t_send, t_recv, n)
 
     def last(n, carry):
         sent(gathered, g_send, g_recv, n)
@@ -428,7 +454,7 @@
     pieces = inner * spans
     bf16 = jnp.bfloat16
     dma = pltpu.SemaphoreType.DMA
-    hops = [dma((2, line_size, G // 2)), dma((line_size, G // 2))]
+    hops = [dma((2, line_size, G)), dma((line_size, G))]
     anywhere = pl.BlockSpec(memory_space=pl.ANY)
     vmem = pl.BlockSpec(memory_space=pltpu.VMEM)
     return pl.pallas_call(
@@ -450,6 +476,7 @@
             pltpu.VMEM((every, HEAD), bf16),
             pltpu.VMEM((every, QC), bf16),
             pltpu.VMEM((2, G, span_size, QC), bf16),
+            pltpu.VMEM((pieces, span_size, QC), jnp.float32),
             dma((3, G)), dma((3, G)), dma((3,)),
             dma((1, G)), dma((1, G)), dma((1,)),
             *hops, *hops,
@@ -570,7 +597,13 @@
     ).astype(jnp.float32)
     marks = jnp.stack([span_start, span_length])
     marks = [marks] + [xor(marks, ki * slices) for ki in range(1, inner)]
-    if learner_rows % 16 == 0 and outer >= 3:
+    if (
+        learner_rows % 16 == 0
+        and outer in (4, 8)
+        and inner * local_spans == KV_HEADS
+        and local_spans >= KV_HEADS // outer
+        and features >= qc
+    ):
         marks = jnp.concatenate(unswap(marks), axis=1)
         cosine, sine = angles(marks[0], span_size)
         cosine, sine = cosine[:, 0], sine[:, 0]

time: 363 us -> 350 us (0.964)
  Pallas kernels: 333 us -> 320 us
    pallas_call x1, Pallas kernels: 333 us -> 320 us  [fused(): pl.pallas_call(functools.partial(body, members, slices, spans, span_size)...]
where the time goes in v4:
time: 350 us; the launch traced here: 344 us
  Pallas kernels  320 us (91%)
  other arithmetic  11.8 us (3%)
  local copies, waits for them, and re-layouts  6.56 us (2%)
  starting transfers between devices  4.89 us (1%)
    pallas_call x1, Pallas kernels, fused(): pl.pallas_call(functools.partial(body, members, slices, spans, span_size)...  320 us
  transfers between devices with their start and end apart: 4, of which 0 were waited for; matrix products, arithmetic and copies ran while one was open for 3% of the time, Pallas kernels for 0%

profile of v4, /device:TPU:0, one launch (start us, length us, event | category | flops | bytes accessed | tf_op | source)
XLA Modules:
  0.0 344.1 jit_solution(3126339524100373736)
XLA Ops:
  0.7 0.7 pad_add_fusion
  1.4 0.5 collective-permute-start.3
  1.8 2.6 collective-permute-start.2
  4.4 0.1 collective-permute-start.1
  4.5 2.3 fusion
  6.8 1.8 collective-permute-start
  8.6 0.8 dynamic_slice.13
  9.4 0.1 dynamic-slice_convert_fusion
  9.5 0.1 dynamic-slice_bitcast_fusion
  9.6 0.6 maximum_convert_fusion.bias
  10.1 0.0 collective-permute-done.3
  10.1 0.0 collective-permute-done.2
  10.2 0.1 pad_add_fusion.1
  10.3 0.5 slice_bitcast_fusion
  10.8 0.1 convert_bitcast_fusion
  10.9 3.7 %fusion.3 = (f32[2048,64]{1,0:T(8,128)S(1)}, f32[2048,64]{1,0:T(8,128)S(1)}, f32[2048,64]{1,0:T(8,128)S(1)}) fusion(f32[64]{0:T(128)S(1)} %negate_power_fusion, f32[2048]{0:T(1024)S(1)} %bitcast.15), kind=kLoop, calls=%fused_computation.9 | loop fusion | flops 262144 | bytes 1581312 | tf_op jit(solution)/shard_map/neg | solution.py:616
  14.6 0.0 copy-start
  14.6 2.0 pad_maximum_fusion
  16.6 0.1 copy-done
  16.7 2.2 fusion.2.normed
  18.9 320.1 %shard_map.130 = (bf16[512,2560]{1,0:T(8,128)(2,1)}, bf16[512,512]{1,0:T(8,128)(2,1)}, bf16[512,512]{1,0:T(8,128)(2,1)}, bf16[8,2048,640]{2,1,0:T(8,128)(2,1)}) custom-call(bf16[512,2560]{1,0:T(8,128)(2,1)} %fusion.2.normed, bf16[160,5120]{1,0:T(8,128)(2,1)} %query_in.1, bf16[160,1024]{1,0:T(8,128)(2,1)} %key_in.1, bf16[160,1024]{1,0:T(8,128)(2,1)} %value_in.1, ...), custom_call_target="tpu_custom_call" | custom-call | tf_op jit(solution)/shard_map/pallas_call | solution.py:460
  339.0 3.5 %copy.18 = bf16[512,2560]{1,0:T(8,128)(2,1)} copy(bf16[512,2560]{1,0:T(8,128)(2,1)} %get-tuple-element.25) | data formatting | bytes 5242880
  342.5 0.8 copy.19
  343.3 0.8 copy.20
  (21 shorter events, 0.1 us)
Async XLA Ops:
  0.6 9.5 %copy-start.4 = (s32[2]{0:T(128)S(1)}, s32[2]{0:T(128)}, u32[]{:S(2)}) copy-start(s32[2]{0:T(128)} %param.21) | copy-start | bytes 28
  0.6 9.5 %copy-start.5 = (s32[2]{0:T(128)S(1)}, s32[2]{0:T(128)}, u32[]{:S(2)}) copy-start(s32[2]{0:T(128)} %param.20) | copy-start | bytes 28
  0.7 8.7 %copy-start.3 = (bf16[5120]{0:T(1024)(128)(2,1)S(1)}, bf16[5120]{0:T(1024)(128)(2,1)}, u32[]{:S(2)}) copy-start(bf16[5120]{0:T(1024)(128)(2,1)} %param.12) | copy-start | bytes 30724
  0.7 8.8 %copy-start.6 = (bf16[512]{0:T(512)(128)(2,1)S(1)}, bf16[512]{0:T(512)(128)(2,1)}, u32[]{:S(2)}) copy-start(bf16[512]{0:T(512)(128)(2,1)} %param.19) | copy-start | bytes 3076
  0.7 8.8 %copy-start.7 = (bf16[512]{0:T(512)(128)(2,1)S(1)}, bf16[512]{0:T(512)(128)(2,1)}, u32[]{:S(2)}) copy-start(bf16[512]{0:T(512)(128)(2,1)} %param.18) | copy-start | bytes 3076
  1.4 8.8 %collective-permute-start.3 = (s32[2,2]{1,0:T(2,128)S(1)}, s32[2,2]{1,0:T(2,128)S(1)}, u32[]{:S(2)}, u32[]{:S(2)}) collective-permute-start(s32[2,2]{1,0:T(2,128)S(1)} %pad_add_fusion), channel_id=1, source_target_pairs={{0,2},{1,3},{2,0},{3,1},{4,6},{5,7},{6,4},{7,5},{8,10},{9,11},{10,... | collective-permute-start | bytes 56 | tf_op jit(solution)/shard_map/ppermute | solution.py:525
  1.8 8.3 %collective-permute-start.2 = (s32[2,2]{1,0:T(2,128)S(1)}, s32[2,2]{1,0:T(2,128)S(1)}, u32[]{:S(2)}, u32[]{:S(2)}) collective-permute-start(s32[2,2]{1,0:T(2,128)S(1)} %pad_add_fusion), channel_id=1, source_target_pairs={{0,4},{1,5},{2,6},{3,7},{4,0},{5,1},{6,2},{7,3},{8,12},{9,13},{10,... | collective-permute-start | bytes 56 | tf_op jit(solution)/shard_map/ppermute | solution.py:525
  4.4 5.8 %collective-permute-start.1 = (s32[2,2]{1,0:T(2,128)S(1)}, s32[2,2]{1,0:T(2,128)S(1)}, u32[]{:S(2)}, u32[]{:S(2)}) collective-permute-start(s32[2,2]{1,0:T(2,128)S(1)} %pad_add_fusion), channel_id=1, source_target_pairs={{0,6},{1,7},{2,4},{3,5},{4,2},{5,3},{6,0},{7,1},{8,14},{9,15},{10,... | collective-permute-start | bytes 56 | tf_op jit(solution)/shard_map/ppermute | solution.py:525
  6.8 9.8 %collective-permute-start = (f32[512,1]{0,1:T(1,128)S(1)}, f32[512,1]{0,1:T(1,128)S(1)}, u32[]{:S(2)}, u32[]{:S(2)}) collective-permute-start(f32[512,1]{0,1:T(1,128)S(1)} %bitcast.17), channel_id=1, source_target_pairs={{0,1},{1,0},{2,3},{3,2},{4,5},{5,4},{6,7},{7,6},{8,9},{9,8},{10,11... | collective-permute-start | bytes 6152 | tf_op jit(solution)/shard_map/ppermute | solution.py:525
  14.6 2.1 copy-start
  339.0 3.5 %copy-start.2 = (bf16[512,512]{1,0:T(8,128)(2,1)S(1)}, bf16[512,512]{1,0:T(8,128)(2,1)}, u32[]{:S(2)}) copy-start(bf16[512,512]{1,0:T(8,128)(2,1)} %get-tuple-element.26) | copy-start | bytes 1572868
  339.0 4.3 %copy-start.1 = (bf16[512,512]{1,0:T(8,128)(2,1)S(1)}, bf16[512,512]{1,0:T(8,128)(2,1)}, u32[]{:S(2)}) copy-start(bf16[512,512]{1,0:T(8,128)(2,1)} %get-tuple-element.27) | copy-start | bytes 1572868
